TPU v7x, 256 devices: a whole 4x4x8 slice. The times are simulated.
256 devices in a mesh: graph: 128 (over y, x, z), mp: 2 (over core).
Axes of the slice: x: 4, y: 4, z: 8, core: 2. Of those that a mesh axis runs over, the one named last changes fastest.
Arguments:
- nodes_in: bfloat16 [262144, 512], P('graph'), may hold values from -24 to 24
- query: bfloat16 [262144, 512], P('graph', 'mp'), may hold values from -200 to 200
- keys: bfloat16 [262144, 512], P('graph', 'mp'), may hold values from -6.5 to 6.5
- values: bfloat16 [262144, 512], P('graph', 'mp'), may hold values from -6 to 6
- grad_attn: bfloat16 [262144, 512], P('graph', 'mp'), may hold values from -6 to 6
- w_query: bfloat16 [512, 512], P(None, 'mp'), may hold values from -0.25 to 0.25
- w_key: bfloat16 [512, 512], P(None, 'mp'), may hold values from -0.25 to 0.25
- w_value: bfloat16 [512, 512], P(None, 'mp'), may hold values from -0.25 to 0.25
- halo_owner: int32 [32768, 1], P('graph'), may hold values from 0 to 127; in each aligned block of 256 rows (0 to 255, 256 to 511, ...) at most 4 rows name the same one
- halo_row: int32 [32768], P('graph'), may hold values from 0 to 2047
- pattern: int32 [2048, 2], P('graph'), may hold values 0 or 1
Outputs:
- grad_nodes: bfloat16 [262144, 512], P('graph', 'mp')
- grad_weights: float32 [512, 3, 512], P('graph', None, 'mp')
Inputs may be any that keep to these rules, and one draw needn't show every extreme that they name: `halo_owner`: among the 256 reads of one partition no owner appears more than 4 times, and some owner appears exactly 4 times.
All inputs are finite; a program needn't handle non-finite values. No bound on the sum of `pattern` on one device may be relied on, other than what follows from the above.
Results may differ from a plain program's by a relative error of at most 0.014.
Values may be sent and summed in bfloat16 or wider, within the bound.
A program may use at most 128 MiB of HBM per device.

v0:
```python
import math

import jax
import jax.numpy as jnp
from jax import lax
from jax.sharding import PartitionSpec as P

D = 512
HEADS = 8
BLK = 128


def attend_blocks(queries_b, keys_b, values_b, douts_b, halo_keys, halo_values, visible, scale):
    wide = jnp.float32
    scores_own = (
        jnp.einsum("bqhe,bkhe->bhqk", queries_b, keys_b, preferred_element_type=wide) * scale
    )
    scores_far = (
        jnp.einsum("bqhe,khe->bhqk", queries_b, halo_keys, preferred_element_type=wide) * scale
    )
    scores_far = jnp.where(visible, scores_far, -1e30)
    highest = jnp.maximum(
        jnp.max(scores_own, -1, keepdims=True), jnp.max(scores_far, -1, keepdims=True)
    )
    weight_own = jnp.exp(scores_own - highest)
    weight_far = jnp.where(visible, jnp.exp(scores_far - highest), 0.0)
    totals = jnp.sum(weight_own, -1, keepdims=True) + jnp.sum(weight_far, -1, keepdims=True)
    prob_own = weight_own / totals
    prob_far = weight_far / totals
    dprob_own = jnp.einsum("bqhe,bkhe->bhqk", douts_b, values_b, preferred_element_type=wide)
    dprob_far = jnp.einsum("bqhe,khe->bhqk", douts_b, halo_values, preferred_element_type=wide)
    row_term = jnp.sum(prob_own * dprob_own, -1, keepdims=True) + jnp.sum(
        prob_far * dprob_far, -1, keepdims=True
    )
    slope_own = (prob_own * (dprob_own - row_term)).astype(jnp.bfloat16)
    slope_far = (prob_far * (dprob_far - row_term)).astype(jnp.bfloat16)
    low_own = prob_own.astype(jnp.bfloat16)
    low_far = prob_far.astype(jnp.bfloat16)
    grad_q = scale * (
        jnp.einsum("bhqk,bkhe->bqhe", slope_own, keys_b, preferred_element_type=wide)
        + jnp.einsum("bhqk,khe->bqhe", slope_far, halo_keys, preferred_element_type=wide)
    )
    grad_k_own = scale * jnp.einsum(
        "bhqk,bqhe->bkhe", slope_own, queries_b, preferred_element_type=wide
    )
    grad_k_far = scale * jnp.einsum(
        "bhqk,bqhe->khe", slope_far, queries_b, preferred_element_type=wide
    )
    grad_v_own = jnp.einsum("bhqk,bqhe->bkhe", low_own, douts_b, preferred_element_type=wide)
    grad_v_far = jnp.einsum("bhqk,bqhe->khe", low_far, douts_b, preferred_element_type=wide)
    return (grad_q, grad_k_own, grad_v_own, grad_k_far, grad_v_far)


def on_device(
    nodes_in, query, keys, values, grad_attn, w_query, w_key, w_value, halo_owner, halo_row, pattern
):
    parts = lax.axis_size("graph")
    rows_dev, width_local = query.shape
    width_full = nodes_in.shape[1]
    halo_len = halo_row.shape[0]
    head_size = D // HEADS
    heads_local = width_local // head_size
    blocks_dev = rows_dev // BLK
    capacity = 2 * halo_len // parts
    scale = 1.0 / math.sqrt(head_size)
    owners = halo_owner[:, 0]
    onehot = (owners[:, None] == jnp.arange(parts, dtype=jnp.int32)[None, :]).astype(jnp.int32)
    ranks = jnp.sum(jnp.cumsum(onehot, 0) * onehot, 1) - 1
    position = owners * capacity + ranks
    wanted = (
        jnp.zeros((parts * capacity,), jnp.int32)
        .at[position]
        .set(halo_row)
        .reshape(parts, capacity)
    )
    asked = lax.all_to_all(wanted, "graph", split_axis=0, concat_axis=0, tiled=True)
    asked_flat = asked.reshape(parts * capacity)
    paired = jnp.concatenate([keys, values], 1)
    outgoing = paired[asked_flat].reshape(parts, capacity, 2 * width_local)
    arrived = lax.all_to_all(outgoing, "graph", split_axis=0, concat_axis=0, tiled=True)
    halo = arrived.reshape(parts * capacity, 2 * width_local)[position]
    shape_blocks = (blocks_dev, BLK, heads_local, head_size)
    shape_halo = (halo_len, heads_local, head_size)
    visible = (jnp.repeat(pattern, BLK, axis=1) > 0)[:, None, None, :]
    outputs = attend_blocks(
        query.reshape(shape_blocks),
        keys.reshape(shape_blocks),
        values.reshape(shape_blocks),
        grad_attn.reshape(shape_blocks),
        halo[:, :width_local].reshape(shape_halo),
        halo[:, width_local:].reshape(shape_halo),
        visible,
        scale,
    )
    grad_q, grad_k_own, grad_v_own, grad_k_far, grad_v_far = outputs
    far_pair = jnp.concatenate(
        [grad_k_far.reshape(halo_len, width_local), grad_v_far.reshape(halo_len, width_local)], 1
    )
    returning = (
        jnp.zeros((parts * capacity, 2 * width_local), jnp.float32).at[position].set(far_pair)
    )
    returned = lax.all_to_all(
        returning.reshape(parts, capacity, 2 * width_local).astype(jnp.bfloat16),
        "graph",
        split_axis=0,
        concat_axis=0,
        tiled=True,
    ).astype(jnp.float32)
    added = (
        jnp.zeros((rows_dev, 2 * width_local), jnp.float32)
        .at[asked_flat]
        .add(returned.reshape(parts * capacity, 2 * width_local))
    )
    grad_query = grad_q.reshape(rows_dev, width_local).astype(jnp.bfloat16)
    grad_key = (grad_k_own.reshape(rows_dev, width_local) + added[:, :width_local]).astype(
        jnp.bfloat16
    )
    grad_value = (grad_v_own.reshape(rows_dev, width_local) + added[:, width_local:]).astype(
        jnp.bfloat16
    )
    stacked = jnp.concatenate([grad_query, grad_key, grad_value], 1)
    product = jnp.einsum("nd,nf->df", nodes_in, stacked, preferred_element_type=jnp.float32)
    grad_weights = lax.psum_scatter(
        product.reshape(width_full // parts * lax.axis_size("graph"), 3, width_local),
        "graph",
        scatter_dimension=0,
        tiled=True,
    )
    joined = jnp.concatenate([w_query, w_key, w_value], 1)
    partial_terms = jnp.einsum("nf,df->nd", stacked, joined, preferred_element_type=jnp.float32)
    grad_nodes = lax.psum_scatter(
        partial_terms.astype(jnp.bfloat16), "mp", scatter_dimension=1, tiled=True
    )
    return (grad_nodes, grad_weights)


def solution(mesh):
    in_specs = (
        P("graph", None),
        P("graph", "mp"),
        P("graph", "mp"),
        P("graph", "mp"),
        P("graph", "mp"),
        P(None, "mp"),
        P(None, "mp"),
        P(None, "mp"),
        P("graph", None),
        P("graph"),
        P("graph", None),
    )
    out_specs = (P("graph", "mp"), P("graph", None, "mp"))
    return jax.shard_map(
        on_device, mesh=mesh, in_specs=in_specs, out_specs=out_specs, check_vma=False
    )
```

profile of v0, /device:TPU:2, one launch (start us, length us, event | category | flops | bytes accessed | tf_op | source)
XLA Modules:
  0.0 436.8 jit_solution(12470529760833313540)
XLA Ops:
  8.0 0.9 copy.200
  8.9 0.2 fusion.48
  9.3 0.9 fusion.49
  10.1 0.7 compare_select_fusion.1
  10.8 1.6 scatter_custom_fusion
  12.4 0.7 all_to_all.12
  13.1 15.4 %all-to-all-start = ((s32[128,1,4]{2,1,0:T(1,128)}), s32[128,1,4]{2,1,0:T(1,128)S(1)}, u32[]{:S(2)}, u32[]{:S(2)}) async-start(s32[128,1,4]{2,1,0:T(1,128)} %bitcast.7), calls=%async_computation | async-start | bytes 131072 | tf_op jit(solution)/shard_map/all_to_all | solution.py:76
  28.5 3.0 pad_maximum_fusion.1
  31.6 7.9 %all-to-all-done = s32[128,1,4]{2,1,0:T(1,128)S(1)} async-done(((s32[128,1,4]{2,1,0:T(1,128)}), s32[128,1,4]{2,1,0:T(1,128)S(1)}, u32[]{:S(2)}, u32[]{:S(2)}) %all-to-all-start) | async-done | bytes 2080 | tf_op jit(solution)/shard_map/all_to_all | solution.py:76
  39.5 0.5 broadcast.108
  40.0 0.8 reduce.3
  41.0 4.5 %gather_fusion = bf16[512,512]{1,0:T(8,128)(2,1)} fusion(bf16[2048,512]{1,0:T(8,128)(2,1)} %pad_maximum_fusion.1, s32[1024]{0:T(1024)S(1)} %pad_clamp_fusion.1), kind=kCustom, calls=%fused_computation | custom fusion | bytes 1050624 | tf_op jit(solution)/shard_map/gather | solution.py:79
  45.5 2.0 reshape.144
  47.5 8.5 %all-to-all-start.1 = ((bf16[128,4,512]{2,1,0:T(4,128)(2,1)}), bf16[128,4,512]{2,1,0:T(4,128)(2,1)}, u32[]{:S(2)}, u32[]{:S(2)}) async-start(bf16[128,4,512]{2,1,0:T(4,128)(2,1)} %reshape.144), calls=%async_computation.1 | async-start | bytes 1048576 | tf_op jit(solution)/shard_map/all_to_all | solution.py:80
  56.0 1.9 reshape.210
  57.8 4.4 %reshape.203 = bf16[16,128,4,64]{3,2,1,0:T(4,128)(2,1)} reshape(bf16[2048,256]{1,0:T(8,128)(2,1)} %param.14) | data formatting | bytes 2097152 | tf_op jit(solution)/shard_map/reshape | solution.py:88
  62.5 2.3 copy.195
  64.7 1.4 copy.260
  66.2 3.9 copy.198
  70.1 2.3 copy.209
  72.4 2.4 copy.262
  74.8 4.8 %multiply_reduce_fusion.1 = (f32[16,4,128]{2,1,0:T(4,128)}, f32[16,4,128,128]{2,3,1,0:T(8,128)}) fusion(bf16[16,128,4,64]{1,3,2,0:T(8,128)(2,1)} %copy.198, bf16[16,128,4,64]{1,0,3,2:T(8,128)(2,1)S(1)} %bitcast.108), kind=kOutput, calls=%fused_computation.22 | convolution fusion | flops 136306688 | bytes 6324224 | tf_op jit(solution)/shard_map/bqhe,bkhe->bhqk/dot_general | solution.py:16
  79.6 2.0 reshape.145
  81.6 2.3 gather_fusion.1
  83.9 0.7 fusion.58
  84.6 1.0 copy.203
  85.6 2.9 fusion.3
  88.6 2.5 fusion.5
  91.1 0.7 copy-done.1
  91.7 0.8 copy.213
  92.5 3.3 fusion.11
  95.9 6.8 %fusion.8 = f32[4,256,64,1]{1,2,3,0:T(8,128)} fusion(bf16[16,128,4,64]{1,0,3,2:T(8,128)(2,1)S(1)} %bitcast.117, f32[4,256,16,128]{3,1,2,0:T(8,128)} %copy-done.1, f32[16,4,128]{2,0,1:T(8,128)S(1)} %copy_add_fusion.1, f32[16,4,128]{2,0,1:T(8,128)S(1)} %copy_maximum_fusion, pred[16,256]{1,0:T(8,128)(4,1)S(1)} %bitcast.128), kind=kOutput, calls=%fused_computation.17 | convolution fusion | flops 281018368 | bytes 9768960 | tf_op jit(solution)/shard_map/bhqk,bqhe->khe/dot_general | solution.py:50
  102.7 4.6 %fusion = (f32[16,4,128]{2,0,1:T(8,128)S(1)}, f32[4,256,16,128]{3,1,2,0:T(8,128)S(1)}) fusion(f32[16,4,128]{2,0,1:T(8,128)S(1)} %copy_add_fusion.1, f32[16,4,128]{2,0,1:T(8,128)S(1)} %copy_maximum_fusion, f32[4,256,16,128]{3,1,2,0:T(8,128)S(1)} %bitcast.107, pred[16,256]{1,0:T(8,128)(4,1)S(1)} %bitcast.129, bf16[256,4,64,1]{0,2,3,1:T(8,128)(2,1)S(1)} %bitcast.125, ...), kind=kOutput, calls=%fused_computation.7 | convolution fusion | flops 283107328 | bytes 18059264 | tf_op jit(solution)/shard_map/bqhe,khe->bhqk/dot_general | solution.py:31
  107.4 3.4 multiply_reduce_fusion
  110.8 3.7 fusion.2
  114.5 2.1 fusion.26
  116.6 0.9 fusion.6
  117.5 1.3 copy-done.5
  118.8 1.7 multiply_convert_fusion
  120.5 1.3 copy-done.3
  121.8 1.7 fusion.15
  123.5 4.1 copy.250
  127.5 4.4 reshape.204
  131.9 1.1 copy.228
  133.0 1.8 copy.229
  134.7 2.9 scatter_custom_fusion.1
  137.6 2.1 convert_element_type.45
  139.7 2.0 convert_element_type.46
  141.6 14.3 %all-to-all-start.2 = ((bf16[128,4,512]{2,1,0:T(4,128)(2,1)}), bf16[128,4,512]{2,1,0:T(4,128)(2,1)}, u32[]{:S(2)}, u32[]{:S(2)}) async-start(bf16[128,4,512]{2,1,0:T(4,128)(2,1)} %convert_element_type.46), calls=%async_computation.2 | async-start | bytes 1048576 | tf_op jit(solution)/shard_map/all_to_all | solution.py:102
  156.0 4.5 %multiply_bitcast_fusion = f32[16,128,4,64]{1,3,2,0:T(8,128)} fusion(bf16[16,4,128,128]{2,3,1,0:T(8,128)(2,1)} %copy-done.3, bf16[16,128,4,64]{1,0,3,2:T(8,128)(2,1)S(1)} %bitcast.111), kind=kOutput, calls=%fused_computation.41 | convolution fusion | flops 134742016 | bytes 5242880 | tf_op jit(solution)/shard_map/bhqk,bqhe->bkhe/dot_general | solution.py:43
  160.5 5.0 %copy.251 = f32[16,128,4,64]{3,2,1,0:T(4,128)} copy(f32[16,128,4,64]{1,3,2,0:T(8,128)} %multiply_bitcast_fusion) | data formatting | bytes 4194304 | tf_op jit(solution)/shard_map/reshape | solution.py:115
  165.5 5.4 %reshape.205 = f32[2048,256]{1,0:T(8,128)} reshape(f32[16,128,4,64]{3,2,1,0:T(4,128)} %copy.251) | data formatting | bytes 4194304 | tf_op jit(solution)/shard_map/reshape | solution.py:115
  170.8 5.1 %fusion.22 = f32[16,128,4,64]{1,3,2,0:T(8,128)} fusion(bf16[16,128,4,64]{1,0,3,2:T(8,128)(2,1)S(1)} %bitcast.120, f32[16,4,128,128]{2,3,1,0:T(8,128)} %get-tuple-element.9, f32[16,4,128]{2,1,0:T(4,128)S(1)} %copy.208, f32[16,4,128]{2,1,0:T(4,128)S(1)} %copy-done.14), kind=kOutput, calls=%fused_computation.42 | convolution fusion | flops 138412032 | bytes 7405568 | tf_op jit(solution)/shard_map/bhqk,bqhe->bkhe/dot_general | solution.py:49
  175.9 4.8 %copy.252 = f32[16,128,4,64]{3,2,1,0:T(4,128)} copy(f32[16,128,4,64]{1,3,2,0:T(8,128)} %fusion.22) | data formatting | bytes 4194304 | tf_op jit(solution)/shard_map/reshape | solution.py:118
  180.7 5.3 %reshape.206 = f32[2048,256]{1,0:T(8,128)} reshape(f32[16,128,4,64]{3,2,1,0:T(4,128)} %copy.252) | data formatting | bytes 4194304 | tf_op jit(solution)/shard_map/reshape | solution.py:118
  186.0 1.1 reshape.195
  187.1 5.7 %scatter_custom_fusion.2 = f32[2048,512]{1,0:T(8,128)} fusion(s32[512]{0:T(512)S(1)} %bitcast.136, f32[512,512]{1,0:T(8,128)S(1)} %reshape.195, f32[]{:T(128)} %constant.17.clone.1), kind=kCustom, calls=%fused_computation.39 | custom fusion | flops 262144 | bytes 4194308 | tf_op jit(solution)/shard_map/scatter-add | solution.py:112
  192.8 4.0 fusion.13
  196.8 3.0 fusion.25
  199.8 3.1 copy.236
  203.0 4.8 %convolution_convert_fusion = bf16[2048,512]{1,0:T(8,128)(2,1)} fusion(bf16[2048,256]{1,0:T(8,128)(2,1)} %copy-done.10, bf16[2048,256]{1,0:T(8,128)(2,1)} %copy-done.9, bf16[2048,256]{1,0:T(8,128)(2,1)S(1)} %copy-done.8, bf16[512,256]{1,0:T(8,128)(2,1)S(1)} %copy-done.17, bf16[512,256]{1,0:T(8,128)(2,1)} %param.17, bf16[512,256]{1,0:T(8,128)(2,1)} %param.16), kind=kOutput, calls=%fused_computation.26 | convolution fusion | flops 1623457792 | bytes 6029312 | tf_op jit(solution)/shard_map/nf,df->nd/dot_general | solution.py:130
  207.9 0.6 dynamic-slice
  209.1 218.7 %all-reduce.3.cloned.1.call-done = f32[512,3,256]{2,0,1:T(8,128)} async-done(((f32[512,3,256]{2,0,1:T(8,128)}), f32[512,3,256]{2,0,1:T(8,128)}) %all-reduce.3.cloned.1.call-update) | async-done | bytes 1572880
  427.8 1.3 constant_dynamic-slice_fusion
  (70 shorter events, 0.7 us)
Async XLA Ops:
  8.0 188.8 %copy-start = (bf16[2048,512]{1,0:T(8,128)(2,1)S(1)}, bf16[2048,512]{1,0:T(8,128)(2,1)}, u32[]{:S(2)}) copy-start(bf16[2048,512]{1,0:T(8,128)(2,1)} %param.11) | copy-start | bytes 6291460
  13.1 26.4 %all-to-all-start = ((s32[128,1,4]{2,1,0:T(1,128)}), s32[128,1,4]{2,1,0:T(1,128)S(1)}, u32[]{:S(2)}, u32[]{:S(2)}) async-start(s32[128,1,4]{2,1,0:T(1,128)} %bitcast.7), calls=%async_computation | async-start | bytes 131072 | tf_op jit(solution)/shard_map/all_to_all | solution.py:76
  31.6 24.4 %copy-start.6 = (bf16[2048,256]{1,0:T(8,128)(2,1)S(1)}, bf16[2048,256]{1,0:T(8,128)(2,1)}, u32[]{:S(2)}) copy-start(bf16[2048,256]{1,0:T(8,128)(2,1)} %param.13) | copy-start | bytes 3145732
  45.5 16.8 %copy-start.18 = (s32[16,2]{0,1:T(2,128)S(1)}, s32[16,2]{0,1:T(2,128)}, u32[]{:S(2)}) copy-start(s32[16,2]{0,1:T(2,128)} %param.21) | copy-start | bytes 388
  47.5 32.1 %all-to-all-start.1 = ((bf16[128,4,512]{2,1,0:T(4,128)(2,1)}), bf16[128,4,512]{2,1,0:T(4,128)(2,1)}, u32[]{:S(2)}, u32[]{:S(2)}) async-start(bf16[128,4,512]{2,1,0:T(4,128)(2,1)} %reshape.144), calls=%async_computation.1 | async-start | bytes 1048576 | tf_op jit(solution)/shard_map/all_to_all | solution.py:80
  85.6 3.0 copy-start.15
  88.5 3.2 copy-start.1
  88.6 28.9 %copy-start.13 = (f32[16,4,128]{2,1,0:T(4,128)}, f32[16,4,128]{2,1,0:T(4,128)S(1)}, u32[]{:S(2)}) copy-start(f32[16,4,128]{2,1,0:T(4,128)S(1)} %copy.206) | copy-start | bytes 98308
  92.5 3.3 copy-start.11
  92.5 10.2 %slice-start = ((s8[8388608]{0:T(1024)(128)(4,1)}), s8[4194304]{0:T(1024)(128)(4,1)S(1)}, s32[]{:S(2)}) async-start(s8[8388608]{0:T(1024)(128)(4,1)} %bitcast.106), calls=%async_computation.6 | async-start | bytes 8388608
  95.9 6.9 %slice-start.1 = ((s8[8388608]{0:T(1024)(128)(4,1)}), s8[4194304]{0:T(1024)(128)(4,1)S(1)}, s32[]{:S(2)}) async-start(s8[8388608]{0:T(1024)(128)(4,1)} %bitcast.106), calls=%async_computation.7 | async-start | bytes 8388608
  95.9 6.8 %copy-start.16 = (bf16[256,256]{0,1:T(8,128)(2,1)S(1)}, bf16[256,256]{0,1:T(8,128)(2,1)}, u32[]{:S(2)}) copy-start(bf16[256,256]{0,1:T(8,128)(2,1)} %copy.213) | copy-start | bytes 393220
  102.7 4.7 %copy-start.2 = (f32[16,4,128,128]{2,3,1,0:T(8,128)S(1)}, f32[16,4,128,128]{2,3,1,0:T(8,128)}, u32[]{:S(2)}) copy-start(f32[16,4,128,128]{2,3,1,0:T(8,128)} %get-tuple-element.9) | copy-start | bytes 12582916
  102.7 4.7 %copy-start.7 = (bf16[16,128,4,64]{3,2,1,0:T(4,128)(2,1)S(1)}, bf16[16,128,4,64]{3,2,1,0:T(4,128)(2,1)}, u32[]{:S(2)}) copy-start(bf16[16,128,4,64]{3,2,1,0:T(4,128)(2,1)} %reshape.203) | copy-start | bytes 3145732
  116.6 2.2 copy-start.5
  118.8 3.0 copy-start.4
  120.4 1.4 copy-start.3
  141.6 44.3 %all-to-all-start.2 = ((bf16[128,4,512]{2,1,0:T(4,128)(2,1)}), bf16[128,4,512]{2,1,0:T(4,128)(2,1)}, u32[]{:S(2)}, u32[]{:S(2)}) async-start(bf16[128,4,512]{2,1,0:T(4,128)(2,1)} %convert_element_type.46), calls=%async_computation.2 | async-start | bytes 1048576 | tf_op jit(solution)/shard_map/all_to_all | solution.py:102
  156.0 271.8 %all-reduce.3.cloned.1.call-start = ((), (), s32[]{:S(2)}) async-start(), calls=%async_computation.5 | async-start | bytes 3145728
  165.5 5.4 %copy-start.12 = (bf16[32,8,16,128]{3,2,1,0:T(8,128)(2,1)S(1)}, bf16[32,8,16,128]{3,2,1,0:T(8,128)(2,1)}, u32[]{:S(2)}) copy-start(bf16[32,8,16,128]{3,2,1,0:T(8,128)(2,1)} %copy.262) | copy-start | bytes 3145732
  165.5 5.4 %copy-start.14 = (f32[16,4,128]{2,1,0:T(4,128)S(1)}, f32[16,4,128]{2,1,0:T(4,128)}, u32[]{:S(2)}) copy-start(f32[16,4,128]{2,1,0:T(4,128)} %copy-done.13) | copy-start | bytes 98308
  192.8 4.0 copy-start.8
  196.8 3.0 copy-start.9
  196.8 3.0 copy-start.10
  199.8 3.2 copy-start.17
  202.9 5.0 %copy-start.19 = (u32[256]{0:T(256)S(1)}, u32[256]{0:T(256)}, u32[]{:S(2)}) copy-start(u32[256]{0:T(256)} %constant.7) | copy-start | bytes 3076
  202.9 226.2 %reduce-scatter.3.cloned.1.call-start = ((), (), s32[]{:S(2)}) async-start(), calls=%async_computation.4 | async-start | bytes 3145728 | tf_op jit(solution)/shard_map/reduce_scatter | solution.py:131
Sparse Core Ops, SparseCore 0:
  203.0 224.7 all-reduce.2
Sparse Core Ops, SparseCore 1:
  207.9 16.2 reduce-scatter.2
where the time goes:
time: 444 us; the launch traced here: 437 us
  waiting for transfers between devices  227 us (51%)
  local copies, waits for them, and re-layouts  79.1 us (18%)
  matrix products  44.5 us (10%)
  starting transfers between devices  38.3 us (9%)
  other arithmetic  31.4 us (7%)
  between operations  16.8 us (4%)
    unnamed x3, waiting for transfers between devices  219 us
    all_to_all x1, starting transfers between devices, on_device(): lax.all_to_all(wanted, 'graph', split_axis=0, concat_axis=0, tiled=True)  15.4 us
    all_to_all x1, starting transfers between devices, on_device(): lax.all_to_all(returning.reshape(parts, capacity, 2 * width_local).astype...  14.3 us
    unnamed x52, local copies, waits for them, and re-layouts  13.8 us
    reshape x2, local copies, waits for them, and re-layouts, on_device(): grad_k_own.reshape(rows_dev, width_local) + added[:, :width_local]  10.3 us
    reshape x2, local copies, waits for them, and re-layouts, on_device(): grad_v_own.reshape(rows_dev, width_local) + added[:, width_local:]  10 us
  transfers between devices with their start and end apart: 5, of which 2 were waited for; matrix products, arithmetic and copies ran while one was open for 15% of the time, Pallas kernels for 0%

commit v1 on v0

v1 whole, which is shorter than its diff:
```python
import functools
import math

import jax
import jax.numpy as jnp
from jax import lax
from jax.experimental import pallas as pl
from jax.experimental.pallas import tpu as pltpu
from jax.sharding import PartitionSpec as P

MESH = pl.DeviceIdType.MESH
F32 = jnp.float32
BF16 = jnp.bfloat16
I32 = jnp.int32

HEADS_LOCAL = 4
E = 64
BLK = 128
ROWS = 2048
W = 256
HR = 256
CAP = 4
NX, NY, NZ = 4, 4, 8
NG = NX * NY * NZ
NPLANE = NX * NY
HALF = NG // 2
LOG2E = 1.4426950408889634
NT = (((1,), (1,)), ((), ()))
TN = (((0,), (0,)), ((), ()))


def dot(a, b, dims=(((1,), (0,)), ((), ()))):
    return lax.dot_general(a, b, dims, preferred_element_type=F32)


def iota(shape, dim):
    return lax.broadcasted_iota(I32, shape, dim)


def place():
    me = lax.axis_index("graph")
    mp = lax.axis_index("mp")
    return me, mp, lax.div(me, NZ), lax.rem(me, NZ)


def peer(plane, z, dplane, dz):
    return lax.rem(plane + dplane, NPLANE) * NZ + lax.rem(z + dz, NZ)


def peer_back(plane, z, k):
    dplane, dz = lax.div(k, NZ), lax.rem(k, NZ)
    return lax.rem(plane - dplane + NPLANE, NPLANE) * NZ + lax.rem(z - dz + NZ, NZ)


def relative(owner, plane, z):
    dplane = ((owner >> 3) - plane + NPLANE) & (NPLANE - 1)
    dz = ((owner & 7) - z + NZ) & (NZ - 1)
    return dplane, dz


def rank_column(owner_c, owner_r):
    same = (owner_c == owner_r) & (iota((HR, HR), 1) < iota((HR, HR), 0))
    return jnp.sum(jnp.where(same, 1, 0), axis=1, keepdims=True)


def rank_row(owner_c, owner_r):
    same = (owner_c == owner_r) & (iota((HR, HR), 0) < iota((HR, HR), 1))
    return jnp.sum(jnp.where(same, 1, 0), axis=0, keepdims=True)


def onehot(mask):
    return jnp.where(mask, 1.0, 0.0).astype(BF16)


def wait_bytes(ref, sem):
    pltpu.make_async_copy(ref, ref, sem).wait()


def send(src, dst, ssem, rsem, dev):
    pltpu.make_async_remote_copy(
        src_ref=src, dst_ref=dst, send_sem=ssem, recv_sem=rsem, device_id=dev, device_id_type=MESH
    ).start()


def greet_all(me, mp, plane, z):
    barrier = pltpu.get_barrier_semaphore()

    @pl.loop(1, NG)
    def _(k):
        p = peer(plane, z, lax.div(k, NZ), lax.rem(k, NZ))
        pl.semaphore_signal(barrier, inc=1, device_id=(p, mp), device_id_type=MESH)

    pl.semaphore_signal(barrier, inc=1, device_id=(me, 1 - mp), device_id_type=MESH)
    return barrier


def gather_kernel(
    owner_c_ref, owner_r_ref, row_r_ref, keys_hbm, values_hbm, nodes_hbm,
    halo_ref, far_nodes_ref, asked_ref,
    kbuf, vbuf, nbuf, s1, r1, s2, r2, fst, kv_send, kv_recv, n_send, n_recv, stack, other,
    lsem, ssem, rsem,
):
    me, mp, plane, z = place()
    loads = [
        pltpu.make_async_copy(keys_hbm, kbuf, lsem.at[0]),
        pltpu.make_async_copy(values_hbm, vbuf, lsem.at[1]),
        pltpu.make_async_copy(nodes_hbm, nbuf, lsem.at[2]),
    ]
    for load in loads:
        load.start()
    barrier = greet_all(me, mp, plane, z)

    owner_c, owner_r, row_r = owner_c_ref[...], owner_r_ref[...], row_r_ref[...]
    rank_c = rank_column(owner_c, owner_r)
    dplane_c, dz_c = relative(owner_c, plane, z)
    _, dz_r = relative(owner_r, plane, z)
    lane_c = dplane_c * CAP + rank_c
    column = onehot(lane_c == iota((HR, 128), 1))
    value = row_r + 1
    at_z = dz_r == iota((NZ, HR), 0)
    high = jnp.where(at_z, value >> 6, 0).astype(F32).astype(BF16)
    low = jnp.where(at_z, value & 63, 0).astype(F32).astype(BF16)
    wanted = (dot(high, column) * 64.0 + dot(low, column)).astype(I32) - 1
    for dz in range(NZ):
        s1[dz] = jnp.broadcast_to(wanted[dz : dz + 1, :], (8, 128))
    pl.semaphore_wait(barrier, NG)

    for dz in range(1, NZ):
        send(s1.at[dz], r1.at[dz], ssem.at[0], rsem.at[0], (peer(plane, z, 0, dz), mp))
    r1[0] = s1[0]
    wait_bytes(r1.at[pl.ds(0, NZ - 1)], rsem.at[0])
    sub = iota((8, 128), 0)
    gathered = jnp.zeros((8, 128), I32)
    for dz in range(NZ):
        gathered = jnp.where(sub == dz, r1[dz], gathered)
    s2[...] = gathered
    for dp in range(1, NPLANE):
        send(s2, r2.at[dp], ssem.at[1], rsem.at[1], (peer(plane, z, dp, 0), mp))
    r2[0] = gathered
    wait_bytes(r2.at[pl.ds(0, NPLANE - 1)], rsem.at[1])

    table = r2[...].reshape(NG, 128)
    table_t = table.T
    lanes, subs = iota((NG, 128), 1), iota((NG, 128), 0)
    asked = []
    for j in range(CAP):
        asked.append(
            jnp.sum(jnp.where(lanes == (subs >> 3) * CAP + j, table, 0), axis=1, keepdims=True)
        )
        asked_ref[j : j + 1, :] = jnp.sum(
            jnp.where(subs == (lanes >> 3) * CAP + j, table_t, 0), axis=0, keepdims=True
        )
    asked_ref[CAP:8, :] = jnp.zeros((8 - CAP, 128), I32)

    loads[0].wait()
    loads[1].wait()
    for j in range(CAP):
        pick = onehot(asked[j] == iota((NG, ROWS), 1))
        part_k = dot(pick, kbuf[...])
        part_v = dot(pick, vbuf[...])
        for c in range(2):
            fst[pl.ds(4 * j + c, NG, stride=16), :] = part_k[:, c * 128 : (c + 1) * 128]
            fst[pl.ds(4 * j + 2 + c, NG, stride=16), :] = part_v[:, c * 128 : (c + 1) * 128]
    kv_send[...] = fst[...].reshape(NG, 16, 128).astype(BF16)

    @pl.loop(1, NG)
    def _(k):
        p = peer_back(plane, z, k)
        send(kv_send.at[k], kv_recv.at[k], ssem.at[2], rsem.at[2], (p, mp))

    kv_recv[0] = kv_send[0]

    loads[2].wait()
    for j in range(CAP):
        pick = onehot(asked[j] == iota((NG, ROWS), 1))
        part_n = dot(pick, nbuf[...])
        for c in range(4):
            fst[pl.ds(4 * j + c, NG, stride=16), :] = part_n[:, c * 128 : (c + 1) * 128]
    n_send[...] = fst[...].reshape(NG, 16, 128).astype(BF16)

    @pl.loop(1, HALF)
    def _(i):
        k = mp * HALF + i
        p = peer_back(plane, z, k)
        send(n_send.at[k], n_recv.at[i], ssem.at[3], rsem.at[3], (p, mp))

    @pl.when(mp == 1)
    def _():
        p = peer_back(plane, z, HALF)
        send(n_send.at[HALF], n_recv.at[0], ssem.at[4], rsem.at[4], (p, mp))
        wait_bytes(n_recv.at[0], ssem.at[4])
        wait_bytes(n_recv.at[0], rsem.at[4])

    @pl.when(mp == 0)
    def _():
        n_recv[0] = n_send[0]

    wait_bytes(kv_recv.at[pl.ds(0, NG - 1)], rsem.at[2])
    fst[...] = kv_recv[...].astype(F32).reshape(NG * 16, 128)
    for j in range(CAP):
        for c in range(4):
            stack[j * NG : (j + 1) * NG, c * 128 : (c + 1) * 128] = fst[
                pl.ds(4 * j + c, NG, stride=16), :
            ].astype(BF16)
    k_c = dplane_c * NZ + dz_c
    place_mat = onehot(rank_c * NG + k_c == iota((HR, CAP * NG), 1))
    halo_ref[...] = dot(place_mat, stack[...]).astype(BF16)

    wait_bytes(n_recv.at[pl.ds(0, HALF - 1)], rsem.at[3])
    fst[0 : HALF * 16, :] = n_recv[...].astype(F32).reshape(HALF * 16, 128)
    for j in range(CAP):
        for c in range(4):
            stack[j * HALF : (j + 1) * HALF, c * 128 : (c + 1) * 128] = fst[
                pl.ds(4 * j + c, HALF, stride=16), :
            ].astype(BF16)
    k_h = k_c - mp * HALF
    slot = jnp.where((k_h >= 0) & (k_h < HALF), rank_c * HALF + k_h, -1)
    place_half = onehot(slot == iota((HR, CAP * HALF), 1))
    mine = dot(place_half, stack[0 : CAP * HALF, :]).astype(BF16)
    s3 = stack.at[pl.ds(CAP * HALF, HR)]
    s3[...] = mine
    send(s3, other, ssem.at[5], rsem.at[5], (me, 1 - mp))
    wait_bytes(other, rsem.at[5])
    far_nodes_ref[...] = mine + other[...]

    wait_bytes(s1.at[pl.ds(0, NZ - 1)], ssem.at[0])
    wait_bytes(r2.at[pl.ds(0, NPLANE - 1)], ssem.at[1])
    wait_bytes(kv_send.at[pl.ds(0, NG - 1)], ssem.at[2])
    wait_bytes(n_recv.at[pl.ds(0, HALF - 1)], ssem.at[3])
    wait_bytes(other, ssem.at[5])


def attention_kernel(
    pattern_ref, q_ref, k_ref, v_ref, g_ref, n_ref, halo_ref, far_nodes_ref, wq_ref, wk_ref, wv_ref,
    t_ref, gw_ref, mine_ref, other_ref,
    far_kt, far_acc,
):
    step = pl.program_id(0)
    mp = lax.axis_index("mp")
    far_k = halo_ref[:, 0:W]
    far_v = halo_ref[:, W : 2 * W]

    @pl.when(step == 0)
    def _():
        far_kt[...] = (far_k * 0.125).T
        far_acc[...] = jnp.zeros_like(far_acc)
        gw_ref[...] = jnp.zeros_like(gw_ref)

    head_of_lane = iota((BLK, W), 1) // E
    slopes_far, lows_far, queries, grads = [], [], [], []
    for sub in range(2):
        rows = slice(sub * BLK, (sub + 1) * BLK)
        q = q_ref[rows, :] * 0.125
        g = g_ref[rows, :]
        k = k_ref[rows, :]
        v = v_ref[rows, :]
        qm = jnp.concatenate(
            [jnp.where(head_of_lane == h, q, 0.0).astype(BF16) for h in range(HEADS_LOCAL)], 0
        )
        gm = jnp.concatenate(
            [jnp.where(head_of_lane == h, g, 0.0).astype(BF16) for h in range(HEADS_LOCAL)], 0
        )
        bias = [
            jnp.where(pattern_ref[2 * step + sub, h] > 0, 0.0, 1e30).astype(F32) for h in range(2)
        ]
        s_own = dot(k, qm, NT)
        s_far = dot(far_k, qm, NT)
        top = jnp.maximum(
            jnp.max(s_own, 0, keepdims=True),
            jnp.maximum(
                jnp.max(s_far[0:BLK], 0, keepdims=True) - bias[0],
                jnp.max(s_far[BLK:], 0, keepdims=True) - bias[1],
            ),
        )
        p_own = jnp.exp2((s_own - top) * LOG2E)
        p_far = jnp.concatenate(
            [
                jnp.exp2((s_far[0:BLK] - (top + bias[0])) * LOG2E),
                jnp.exp2((s_far[BLK:] - (top + bias[1])) * LOG2E),
            ],
            0,
        )
        total = jnp.sum(p_own, 0, keepdims=True) + jnp.sum(p_far, 0, keepdims=True)
        inv = 1.0 / total
        d_own = dot(v, gm, NT)
        d_far = dot(far_v, gm, NT)
        prob_own = p_own * inv
        prob_far = p_far * inv
        term = jnp.sum(prob_own * d_own, 0, keepdims=True) + jnp.sum(
            prob_far * d_far, 0, keepdims=True
        )
        slope_own = (prob_own * (d_own - term)).astype(BF16)
        slope_far = (prob_far * (d_far - term)).astype(BF16)
        low_own = prob_own.astype(BF16)
        low_far = prob_far.astype(BF16)
        dk = dot(slope_own, qm)
        dv = dot(low_own, gm)
        kt = (k * 0.125).T
        dqt = jnp.concatenate(
            [
                dot(kt[h * E : (h + 1) * E, :], slope_own[:, h * BLK : (h + 1) * BLK])
                + dot(far_kt[h * E : (h + 1) * E, :], slope_far[:, h * BLK : (h + 1) * BLK])
                for h in range(HEADS_LOCAL)
            ],
            0,
        )
        dq = dqt.T
        grads.append((dq.astype(BF16), dk.astype(BF16), dv.astype(BF16)))
        slopes_far.append(slope_far)
        lows_far.append(low_far)
        queries.append((qm, gm))

    slope2 = jnp.concatenate(slopes_far, 1)
    low2 = jnp.concatenate(lows_far, 1)
    qm2 = jnp.concatenate([a for a, _ in queries], 0)
    gm2 = jnp.concatenate([b for _, b in queries], 0)
    far_acc[:, 0:W] += dot(slope2, qm2)
    far_acc[:, W : 2 * W] += dot(low2, gm2)

    nodes = n_ref[...]
    mine = jnp.zeros((2 * BLK, W), F32)
    other = jnp.zeros((2 * BLK, W), F32)
    mine_rows = pl.ds(pl.multiple_of(mp * W, W), W)
    other_rows = pl.ds(pl.multiple_of((1 - mp) * W, W), W)
    for i, w_ref in enumerate((wq_ref, wk_ref, wv_ref)):
        grad = jnp.concatenate([grads[0][i], grads[1][i]], 0)
        gw_ref[:, i * W : (i + 1) * W] += dot(nodes, grad, TN)
        mine += dot(grad, w_ref[mine_rows, :], NT)
        other += dot(grad, w_ref[other_rows, :], NT)
    mine_ref[...] = mine
    other_ref[...] = other.astype(BF16)

    @pl.when(step == pl.num_programs(0) - 1)
    def _():
        dk_far = far_acc[:, 0:W].astype(BF16)
        dv_far = far_acc[:, W : 2 * W].astype(BF16)
        far_nodes = far_nodes_ref[...]
        t_ref[...] = (dot(dk_far, wk_ref[...], NT) + dot(dv_far, wv_ref[...], NT)).astype(BF16)
        gw_ref[:, W : 2 * W] += dot(far_nodes, dk_far, TN)
        gw_ref[:, 2 * W : 3 * W] += dot(far_nodes, dv_far, TN)


def return_kernel(
    owner_c_ref, owner_r_ref, asked_ref, t_ref, gw_hbm, mine_hbm, other_hbm,
    nodes_out, weights_out,
    gw, mine, e_recv, t_recv, fst, z_send, z_recv, x_send, z_full,
    y_send, y_recv, xx_send, xx_recv, zz_send, zz_recv,
    lsem, ssem, rsem,
):
    me, mp, plane, z = place()
    loads = [
        pltpu.make_async_copy(gw_hbm, gw, lsem.at[0]),
        pltpu.make_async_copy(mine_hbm, mine, lsem.at[1]),
    ]
    for load in loads:
        load.start()
    barrier = greet_all(me, mp, plane, z)
    owner_c, owner_r = owner_c_ref[...], owner_r_ref[...]
    rank_r = rank_row(owner_c, owner_r)
    dplane_r, dz_r = relative(owner_r, plane, z)
    k_h = dplane_r * NZ + dz_r - mp * HALF
    slot = jnp.where((k_h >= 0) & (k_h < HALF), rank_r * HALF + k_h, -1)
    place_t = onehot(slot == iota((CAP * HALF, HR), 0))
    pl.semaphore_wait(barrier, NG)

    twin = (me, 1 - mp)
    send(t_ref, t_recv, ssem.at[0], rsem.at[0], twin)
    send(other_hbm, e_recv, ssem.at[1], rsem.at[1], twin)
    loads[0].wait()
    y, x = lax.div(plane, NX), lax.rem(plane, NX)
    y_send[...] = gw[...].astype(BF16).reshape(NY, 128, 3 * W)
    for d in range(1, NY):
        yy = lax.rem(y + d, NY)
        send(y_send.at[yy], y_recv.at[d - 1], ssem.at[2], rsem.at[2], ((yy * NX + x) * NZ + z, mp))

    wait_bytes(t_recv, rsem.at[0])
    summed = (t_ref[...].astype(F32) + t_recv[...].astype(F32)).astype(BF16)
    placed = dot(place_t, summed)
    for j in range(CAP):
        for c in range(4):
            fst[pl.ds(4 * j + c, HALF, stride=16), :] = placed[
                j * HALF : (j + 1) * HALF, c * 128 : (c + 1) * 128
            ]
    z_send[...] = fst[...].reshape(HALF, 16, 128).astype(BF16)

    @pl.loop(1, HALF)
    def _(i):
        k = mp * HALF + i
        p = peer(plane, z, lax.div(k, NZ), lax.rem(k, NZ))
        send(z_send.at[i], z_recv.at[i], ssem.at[3], rsem.at[3], (p, mp))

    @pl.when(mp == 1)
    def _():
        p = peer(plane, z, HALF // NZ, 0)
        send(z_send.at[0], z_recv.at[0], ssem.at[4], rsem.at[4], (p, mp))
        wait_bytes(z_recv.at[0], ssem.at[4])
        wait_bytes(z_recv.at[0], rsem.at[4])

    @pl.when(mp == 0)
    def _():
        z_recv[0] = z_send[0]

    wait_bytes(y_recv, rsem.at[2])
    own = gw[pl.ds(pl.multiple_of(y * 128, 128), 128), :]
    for d in range(NY - 1):
        own += y_recv[d].astype(F32)
    gw[0:128, :] = own
    xx_send[...] = own.astype(BF16).reshape(NX, 32, 3 * W)
    for d in range(1, NX):
        xx = lax.rem(x + d, NX)
        send(xx_send.at[xx], xx_recv.at[d - 1], ssem.at[5], rsem.at[5], ((y * NX + xx) * NZ + z, mp))

    wait_bytes(z_recv.at[pl.ds(0, HALF - 1)], rsem.at[3])
    fst[...] = z_recv[...].astype(F32).reshape(HALF * 16, 128)
    for j in range(CAP):
        for c in range(2):
            x_send[j, :, c * 128 : (c + 1) * 128] = fst[
                pl.ds(4 * j + 2 * (1 - mp) + c, HALF, stride=16), :
            ].astype(BF16)
    send(x_send, z_full.at[:, mp], ssem.at[6], rsem.at[6], twin)
    for j in range(CAP):
        for c in range(2):
            z_full[j, mp, :, c * 128 : (c + 1) * 128] = fst[
                pl.ds(4 * j + 2 * mp + c, HALF, stride=16), :
            ].astype(BF16)

    wait_bytes(xx_recv, rsem.at[5])
    own = gw[pl.ds(pl.multiple_of(x * 32, 32), 32), :]
    for d in range(NX - 1):
        own += xx_recv[d].astype(F32)
    for zz in range(NZ):
        for c in range(6):
            zz_send[zz, 4 * c : 4 * c + 4, :] = own[4 * zz : 4 * zz + 4, c * 128 : (c + 1) * 128]
    for d in range(1, NZ):
        zz = lax.rem(z + d, NZ)
        send(zz_send.at[zz], zz_recv.at[d], ssem.at[7], rsem.at[7], (plane * NZ + zz, mp))
    zz_recv[0] = zz_send[z]

    loads[1].wait()
    wait_bytes(e_recv, rsem.at[1])
    wait_bytes(x_send, rsem.at[6])
    far = z_full[...].reshape(CAP * NG, W)
    chunk = 256

    @pl.loop(0, ROWS // chunk)
    def _(i):
        base = pl.multiple_of(i * chunk, chunk)
        row = iota((chunk, NG), 0) + base
        scatter = jnp.concatenate(
            [onehot(row == asked_ref[j : j + 1, :]) for j in range(CAP)], 1
        )
        rows = pl.ds(base, chunk)
        nodes_out[rows, :] = (
            mine[rows, :] + e_recv[rows, :].astype(F32) + dot(scatter, far)
        ).astype(BF16)

    wait_bytes(zz_recv.at[pl.ds(0, NZ - 1)], rsem.at[7])
    final = zz_recv[0]
    for d in range(1, NZ):
        final += zz_recv[d]
    for r in range(4):
        for c in range(6):
            weights_out[r, c // 2 : c // 2 + 1, (c % 2) * 128 : (c % 2 + 1) * 128] = final[
                4 * c + r : 4 * c + r + 1, :
            ]

    wait_bytes(t_ref, ssem.at[0])
    wait_bytes(e_recv, ssem.at[1])
    wait_bytes(y_recv, ssem.at[2])
    wait_bytes(z_recv.at[pl.ds(0, HALF - 1)], ssem.at[3])
    wait_bytes(xx_recv, ssem.at[5])
    wait_bytes(x_send, ssem.at[6])
    wait_bytes(zz_recv.at[pl.ds(0, NZ - 1)], ssem.at[7])


VM = pl.BlockSpec(memory_space=pltpu.VMEM)
ANY = pl.BlockSpec(memory_space=pl.ANY)
LIMIT = 50 * 1024 * 1024


def on_device(
    nodes_in, query, keys, values, grad_attn, w_query, w_key, w_value, halo_owner, halo_row, pattern
):
    owner_r = halo_owner.reshape(1, HR)
    row_r = halo_row.reshape(1, HR)
    dma = pltpu.SemaphoreType.DMA
    halo, far_nodes, asked = pl.pallas_call(
        gather_kernel,
        out_shape=(
            jax.ShapeDtypeStruct((HR, 2 * W), BF16),
            jax.ShapeDtypeStruct((HR, 2 * W), BF16),
            jax.ShapeDtypeStruct((8, 128), I32),
        ),
        in_specs=[VM, VM, VM, ANY, ANY, ANY],
        out_specs=(VM, VM, VM),
        scratch_shapes=[
            pltpu.VMEM((ROWS, W), BF16),
            pltpu.VMEM((ROWS, W), BF16),
            pltpu.VMEM((ROWS, 2 * W), BF16),
            pltpu.VMEM((NZ, 8, 128), I32),
            pltpu.VMEM((NZ, 8, 128), I32),
            pltpu.VMEM((8, 128), I32),
            pltpu.VMEM((NPLANE, 8, 128), I32),
            pltpu.VMEM((NG * 16, 128), F32),
            pltpu.VMEM((NG, 16, 128), BF16),
            pltpu.VMEM((NG, 16, 128), BF16),
            pltpu.VMEM((NG, 16, 128), BF16),
            pltpu.VMEM((HALF, 16, 128), BF16),
            pltpu.VMEM((CAP * NG, 2 * W), BF16),
            pltpu.VMEM((HR, 2 * W), BF16),
            dma((3,)),
            dma((6,)),
            dma((6,)),
        ],
        compiler_params=pltpu.CompilerParams(
            collective_id=0, has_side_effects=True, vmem_limit_bytes=LIMIT
        ),
        name="gather",
    )(halo_owner, owner_r, row_r, keys, values, nodes_in)

    pair = lambda i: (i, 0)
    whole = lambda i: (0, 0)
    steps = ROWS // (2 * BLK)
    t_part, gw, mine, other = pl.pallas_call(
        attention_kernel,
        grid=(steps,),
        out_shape=(
            jax.ShapeDtypeStruct((HR, 2 * W), BF16),
            jax.ShapeDtypeStruct((2 * W, 3 * W), F32),
            jax.ShapeDtypeStruct((ROWS, W), F32),
            jax.ShapeDtypeStruct((ROWS, W), BF16),
        ),
        in_specs=[
            pl.BlockSpec(memory_space=pltpu.SMEM),
            pl.BlockSpec((2 * BLK, W), pair),
            pl.BlockSpec((2 * BLK, W), pair),
            pl.BlockSpec((2 * BLK, W), pair),
            pl.BlockSpec((2 * BLK, W), pair),
            pl.BlockSpec((2 * BLK, 2 * W), pair),
            pl.BlockSpec((HR, 2 * W), whole),
            pl.BlockSpec((HR, 2 * W), whole),
            pl.BlockSpec((2 * W, W), whole),
            pl.BlockSpec((2 * W, W), whole),
            pl.BlockSpec((2 * W, W), whole),
        ],
        out_specs=(
            pl.BlockSpec((HR, 2 * W), whole),
            pl.BlockSpec((2 * W, 3 * W), whole),
            pl.BlockSpec((2 * BLK, W), pair),
            pl.BlockSpec((2 * BLK, W), pair),
        ),
        scratch_shapes=[pltpu.VMEM((W, HR), BF16), pltpu.VMEM((HR, 2 * W), F32)],
        compiler_params=pltpu.CompilerParams(vmem_limit_bytes=LIMIT),
        name="attention",
    )(pattern, query, keys, values, grad_attn, nodes_in, halo, far_nodes, w_query, w_key, w_value)

    return pl.pallas_call(
        return_kernel,
        out_shape=(
            jax.ShapeDtypeStruct((ROWS, W), BF16),
            jax.ShapeDtypeStruct((4, 3, W), F32),
        ),
        in_specs=[VM, VM, VM, VM, ANY, ANY, ANY],
        out_specs=(VM, VM),
        scratch_shapes=[
            pltpu.VMEM((2 * W, 3 * W), F32),
            pltpu.VMEM((ROWS, W), F32),
            pltpu.VMEM((ROWS, W), BF16),
            pltpu.VMEM((HR, 2 * W), BF16),
            pltpu.VMEM((HALF * 16, 128), F32),
            pltpu.VMEM((HALF, 16, 128), BF16),
            pltpu.VMEM((HALF, 16, 128), BF16),
            pltpu.VMEM((CAP, HALF, W), BF16),
            pltpu.VMEM((CAP, 2, HALF, W), BF16),
            pltpu.VMEM((NY, 128, 3 * W), BF16),
            pltpu.VMEM((NY - 1, 128, 3 * W), BF16),
            pltpu.VMEM((NX, 32, 3 * W), BF16),
            pltpu.VMEM((NX - 1, 32, 3 * W), BF16),
            pltpu.VMEM((NZ, 24, 128), F32),
            pltpu.VMEM((NZ, 24, 128), F32),
            dma((2,)),
            dma((8,)),
            dma((8,)),
        ],
        compiler_params=pltpu.CompilerParams(
            collective_id=1, has_side_effects=True, vmem_limit_bytes=LIMIT
        ),
        name="give_back",
    )(halo_owner, owner_r, asked, t_part, gw, mine, other)


def solution(mesh):
    in_specs = (
        P("graph", None),
        P("graph", "mp"),
        P("graph", "mp"),
        P("graph", "mp"),
        P("graph", "mp"),
        P(None, "mp"),
        P(None, "mp"),
        P(None, "mp"),
        P("graph", None),
        P("graph"),
        P("graph", None),
    )
    out_specs = (P("graph", "mp"), P("graph", None, "mp"))
    return jax.shard_map(
        on_device, mesh=mesh, in_specs=in_specs, out_specs=out_specs, check_vma=False
    )
```

time: 444 us -> 110 us (0.25); the launches traced: 437 us -> 109 us
  waiting for transfers between devices: 227 us -> 0 us
  Pallas kernels: 0 us -> 100 us
  local copies, waits for them, and re-layouts: 79.1 us -> 8.36 us
  matrix products: 44.5 us -> 0 us
  starting transfers between devices: 38.3 us -> 0 us
  other arithmetic: 31.4 us -> 0 us
  between operations: 16.8 us -> 0.72 us
    unnamed x3 -> x0, waiting for transfers between devices: 219 us -> none
    pallas_call x0 -> x3, Pallas kernels: none -> 100 us  [the longest x1 46.2 us: on_device(): pl.pallas_call(gather_kernel, out_shape=(jax.ShapeDtypeStruct((HR, 2 * W)...]
    dot_general x12 -> x0, matrix products: 44.5 us -> none  [the longest x1 6.83 us: attend_blocks(): jnp.einsum('bhqk,bqhe->khe', low_far, douts_b, preferred_element_type=wide)]
    reshape x14 -> x0, local copies, waits for them, and re-layouts: 41.7 us -> none  [the longest x2 10.3 us: on_device(): grad_k_own.reshape(rows_dev, width_local) + added[:, :width_local]]
    all_to_all x3 -> x0, starting transfers between devices: 38.2 us -> none  [the longest x1 15.4 us: on_device(): lax.all_to_all(wanted, 'graph', split_axis=0, concat_axis=0, tiled=True)]
    convert_element_type x4 -> x0, other arithmetic: 11.4 us -> none  [the longest x1 3.99 us: on_device(): (grad_k_own.reshape(rows_dev, width_local) + added[:, :width_local]).asty...]
    convert_element_type x3 -> x0, local copies, waits for them, and re-layouts: 10.4 us -> none  [the longest x2 8.42 us: on_device(): grad_query = grad_q.reshape(rows_dev, width_local).astype(jnp.bfloat16)]
    all_to_all x3 -> x0, waiting for transfers between devices: 7.94 us -> none  [the longest x1 7.94 us: on_device(): lax.all_to_all(wanted, 'graph', split_axis=0, concat_axis=0, tiled=True)]
  transfers between devices with their start and end apart: 5 -> 0, of which waited for: 2 -> 0; matrix products, arithmetic and copies ran while one was open for 15% -> 0% of each run, Pallas kernels for 0% -> 0%
where the time goes in v1:
time: 110 us; the launch traced here: 109 us
  Pallas kernels  100 us (91%)
  local copies, waits for them, and re-layouts  8.36 us (8%)
    pallas_call x1, Pallas kernels, on_device(): pl.pallas_call(gather_kernel, out_shape=(jax.ShapeDtypeStruct((HR, 2 * W)...  46.2 us
    pallas_call x1, Pallas kernels, on_device(): pl.pallas_call(return_kernel, out_shape=(jax.ShapeDtypeStruct((ROWS, W),...  31.7 us
    pallas_call x1, Pallas kernels, on_device(): pl.pallas_call(attention_kernel, grid=(steps,), out_shape=(jax.ShapeDtype...  22.5 us
    unnamed x23, local copies, waits for them, and re-layouts  7.76 us

profile of v1, /device:TPU:2, one launch (start us, length us, event | category | flops | bytes accessed | tf_op | source)
XLA Modules:
  0.0 109.4 jit_solution(8863023650257503217)
XLA Ops:
  0.6 0.8 copy.14.pattern_ref
  1.4 0.8 copy.15.owner_c_ref
  2.2 0.0 copy-start
  2.2 1.2 %copy-done = bf16[2048,256]{1,0:T(8,128)(2,1)S(1)} copy-done((bf16[2048,256]{1,0:T(8,128)(2,1)S(1)}, bf16[2048,256]{1,0:T(8,128)(2,1)}, u32[]{:S(2)}) %copy-start) | copy-done | bytes 1048600
  3.4 0.0 copy-start.1
  3.4 1.2 %copy-done.1 = bf16[2048,256]{1,0:T(8,128)(2,1)S(1)} copy-done((bf16[2048,256]{1,0:T(8,128)(2,1)S(1)}, bf16[2048,256]{1,0:T(8,128)(2,1)}, u32[]{:S(2)}) %copy-start.1) | copy-done | bytes 1048600
  4.7 0.0 copy-start.7
  4.7 0.7 copy-done.7
  5.3 0.0 copy-start.9
  5.3 0.7 copy-done.9
  6.0 0.0 copy-start.3
  6.0 0.0 copy-start.4
  6.0 0.0 copy-start.5
  6.0 0.0 copy-start.6
  6.0 46.2 %gather.1 = (bf16[256,512]{1,0:T(8,128)(2,1)S(1)}, bf16[256,512]{1,0:T(8,128)(2,1)S(1)}, s32[8,128]{1,0:T(8,128)S(1)}) custom-call(s32[256,1]{1,0:T(8,128)S(1)} %copy.15.owner_c_ref, s32[1,256]{1,0:T(1,128)S(1)} %bitcast.2, s32[1,256]{1,0:T(1,128)S(1)} %bitcast.4, bf16[2048,256]{1,0:T(8,128)(2,1)S(1)} %copy-done, bf16[2048,256]{1,0:T(8,128)(2,1)S(1)} %copy-done.1, ...), custom_call_target="tpu_custom_call" | custom-call | tf_op jit(solution)/shard_map/gather/pallas_call | solution.py:487
  52.2 0.0 copy-done.3
  52.2 0.0 copy-done.4
  52.2 0.0 copy-done.5
  52.2 0.0 copy-done.6
  52.3 0.0 copy-start.8
  52.3 22.5 %attention.1 = (bf16[256,512]{1,0:T(8,128)(2,1)S(1)}, f32[512,768]{1,0:T(8,128)}, f32[2048,256]{1,0:T(8,128)}, bf16[2048,256]{1,0:T(8,128)(2,1)S(1)}) custom-call(s32[16,2]{1,0:T(8,128)S(1)} %copy.14.pattern_ref, bf16[2048,256]{1,0:T(8,128)(2,1)S(1)} %copy-done.3, bf16[2048,256]{1,0:T(8,128)(2,1)} %k_ref.1, bf16[2048,256]{1,0:T(8,128)(2,1)} %v_ref.1, ...), custom_call_target="tpu_custom_call" | custom-call | tf_op jit(solution)/shard_map/attention/pallas_call | solution.py:524
  74.8 0.0 copy-done.8
  74.8 0.0 copy-start.2
  74.8 1.4 %copy-done.2 = f32[512,768]{1,0:T(8,128)S(1)} copy-done((f32[512,768]{1,0:T(8,128)S(1)}, f32[512,768]{1,0:T(8,128)}, u32[]{:S(2)}) %copy-start.2) | copy-done | bytes 1572888
  76.2 31.7 %give_back.1 = (bf16[2048,256]{1,0:T(8,128)(2,1)S(1)}, f32[4,3,256]{2,1,0:T(4,128)S(1)}) custom-call(s32[256,1]{1,0:T(8,128)S(1)} %copy.15.owner_c_ref, s32[1,256]{1,0:T(1,128)S(1)} %bitcast.3, s32[8,128]{1,0:T(8,128)S(1)} %get-tuple-element.9.asked_ref, bf16[256,512]{1,0:T(8,128)(2,1)S(1)} %get-tuple-element.12.t_ref, f32[512,768]{1,0:T(8,128)S(1)} %copy-done.2, ...), custom_call_target="tpu_custom_call" | custom-call | tf_op jit(solution)/shard_map/give_back/pallas_call | solution.py:557
  107.9 0.6 copy.16
  108.5 1.0 copy.18
Async XLA Ops:
  2.2 1.2 %copy-start = (bf16[2048,256]{1,0:T(8,128)(2,1)S(1)}, bf16[2048,256]{1,0:T(8,128)(2,1)}, u32[]{:S(2)}) copy-start(bf16[2048,256]{1,0:T(8,128)(2,1)} %k_ref.1) | copy-start | bytes 3145732
  3.4 1.2 %copy-start.1 = (bf16[2048,256]{1,0:T(8,128)(2,1)S(1)}, bf16[2048,256]{1,0:T(8,128)(2,1)}, u32[]{:S(2)}) copy-start(bf16[2048,256]{1,0:T(8,128)(2,1)} %v_ref.1) | copy-start | bytes 3145732
  4.7 0.7 copy-start.7
  5.3 0.7 copy-start.9
  6.0 46.2 %copy-start.3 = (bf16[2048,256]{1,0:T(8,128)(2,1)S(1)}, bf16[2048,256]{1,0:T(8,128)(2,1)}, u32[]{:S(2)}) copy-start(bf16[2048,256]{1,0:T(8,128)(2,1)} %q_ref.1) | copy-start | bytes 3145732
  6.0 46.2 %copy-start.4 = (bf16[512,256]{1,0:T(8,128)(2,1)S(1)}, bf16[512,256]{1,0:T(8,128)(2,1)}, u32[]{:S(2)}) copy-start(bf16[512,256]{1,0:T(8,128)(2,1)} %wq_ref.1) | copy-start | bytes 786436
  6.0 46.2 %copy-start.5 = (bf16[512,256]{1,0:T(8,128)(2,1)S(1)}, bf16[512,256]{1,0:T(8,128)(2,1)}, u32[]{:S(2)}) copy-start(bf16[512,256]{1,0:T(8,128)(2,1)} %wk_ref.1) | copy-start | bytes 786436
  6.0 46.2 %copy-start.6 = (bf16[512,256]{1,0:T(8,128)(2,1)S(1)}, bf16[512,256]{1,0:T(8,128)(2,1)}, u32[]{:S(2)}) copy-start(bf16[512,256]{1,0:T(8,128)(2,1)} %wv_ref.1) | copy-start | bytes 786436
  52.3 22.5 %copy-start.8 = (s32[256,1]{0,1:T(1,128)S(1)}, s32[256,1]{0,1:T(1,128)}, u32[]{:S(2)}) copy-start(s32[256,1]{0,1:T(1,128)} %param.19) | copy-start | bytes 3076
  74.8 1.4 %copy-start.2 = (f32[512,768]{1,0:T(8,128)S(1)}, f32[512,768]{1,0:T(8,128)}, u32[]{:S(2)}) copy-start(f32[512,768]{1,0:T(8,128)} %get-tuple-element.13.gw_hbm) | copy-start | bytes 4718596

commit v2 on v0

v2 whole, which is shorter than its diff:
```python
import functools
import math

import jax
import jax.numpy as jnp
from jax import lax
from jax.experimental import pallas as pl
from jax.experimental.pallas import tpu as pltpu
from jax.sharding import PartitionSpec as P

MESH = pl.DeviceIdType.MESH
F32 = jnp.float32
BF16 = jnp.bfloat16
I32 = jnp.int32

HEADS_LOCAL = 4
E = 64
BLK = 128
ROWS = 2048
W = 256
HR = 256
CAP = 4
NX, NY, NZ = 4, 4, 8
NG = NX * NY * NZ
NPLANE = NX * NY
HALF = NG // 2
LOG2E = 1.4426950408889634
NT = (((1,), (1,)), ((), ()))
TN = (((0,), (0,)), ((), ()))


def dot(a, b, dims=(((1,), (0,)), ((), ()))):
    return lax.dot_general(a, b, dims, preferred_element_type=F32)


def iota(shape, dim):
    return lax.broadcasted_iota(I32, shape, dim)


def place():
    me = lax.axis_index("graph")
    mp = lax.axis_index("mp")
    return me, mp, lax.div(me, NZ), lax.rem(me, NZ)


def peer(plane, z, dplane, dz):
    return lax.rem(plane + dplane, NPLANE) * NZ + lax.rem(z + dz, NZ)


def relative(owner, plane, z):
    dplane = ((owner >> 3) - plane + NPLANE) & (NPLANE - 1)
    dz = ((owner & 7) - z + NZ) & (NZ - 1)
    return dplane, dz


def rank_column(owner_c, owner_r):
    same = (owner_c == owner_r) & (iota((HR, HR), 1) < iota((HR, HR), 0))
    return jnp.sum(jnp.where(same, 1, 0), axis=1, keepdims=True)


def rank_row(owner_c, owner_r):
    same = (owner_c == owner_r) & (iota((HR, HR), 0) < iota((HR, HR), 1))
    return jnp.sum(jnp.where(same, 1, 0), axis=0, keepdims=True)


def onehot(mask):
    return jnp.where(mask, 1.0, 0.0).astype(BF16)


def wait_bytes(ref, sem):
    pltpu.make_async_copy(ref, ref, sem).wait()


def send(src, dst, ssem, rsem, dev):
    pltpu.make_async_remote_copy(
        src_ref=src, dst_ref=dst, send_sem=ssem, recv_sem=rsem, device_id=dev, device_id_type=MESH
    ).start()


def head_stack(x):
    head_of_lane = iota((BLK, W), 1) // E
    return jnp.concatenate(
        [jnp.where(head_of_lane == h, x, 0.0).astype(BF16) for h in range(HEADS_LOCAL)], 0
    )


def layer_kernel(
    pattern_ref, owner_ref, row_ref,
    query_hbm, keys_hbm, values_hbm, grad_hbm, nodes_hbm, wq_hbm, wk_hbm, wv_hbm,
    nodes_out, weights_out,
    qbuf, kbuf, vbuf, gbuf, nbuf, wbuf, obuf,
    s1, r1, s2, r2, fst, kv_send, kv_recv, n_send, n_recv, stack, fn_send, fn_recv,
    asked_ref, far_kv, far_kt, far_acc, pbuf, dbuf, stats, gw, mine, e_send, e_recv,
    t_send, t_recv, fst2, z_send, z_recv, x_send, z_full,
    y_send, y_recv, xx_send, xx_recv, zz_send, zz_recv,
    lsem, osem, ssem, rsem,
):
    me, mp, plane, z = place()
    y, x = lax.div(plane, NX), lax.rem(plane, NX)
    twin = (me, 1 - mp)
    loads = [
        pltpu.make_async_copy(src, dst, lsem.at[i])
        for i, (src, dst) in enumerate(
            (
                (keys_hbm, kbuf),
                (values_hbm, vbuf),
                (query_hbm, qbuf),
                (grad_hbm, gbuf),
                (nodes_hbm, nbuf),
                (wq_hbm, wbuf.at[0]),
                (wk_hbm, wbuf.at[1]),
                (wv_hbm, wbuf.at[2]),
            )
        )
    ]
    for load in loads:
        load.start()
    z_up = [lax.rem(z + d, NZ) for d in range(NZ)]
    z_down = [lax.rem(z - d + NZ, NZ) for d in range(NZ)]

    barrier = pltpu.get_barrier_semaphore()
    for d in range(1, NZ):
        pl.semaphore_signal(barrier, inc=1, device_id=(plane * NZ + z_up[d], mp), device_id_type=MESH)
    for d in range(1, NPLANE):
        pl.semaphore_signal(barrier, inc=1, device_id=(peer(plane, z, d, 0), mp), device_id_type=MESH)
    pl.semaphore_signal(barrier, inc=1, device_id=twin, device_id_type=MESH)

    owner_r, row_r = owner_ref[...], row_ref[...]
    owner_c = jnp.broadcast_to(owner_r, (HR, HR)).T
    rank_c = rank_column(owner_c, owner_r)
    rank_r = rank_row(owner_c, owner_r)
    dplane_c, dz_c = relative(owner_c[:, 0:1], plane, z)
    dplane_r, dz_r = relative(owner_r, plane, z)
    column = onehot(dplane_c * CAP + rank_c == iota((HR, 128), 1))
    value = row_r + 1
    at_z = dz_r == iota((NZ, HR), 0)
    high = jnp.where(at_z, value >> 6, 0).astype(F32).astype(BF16)
    low = jnp.where(at_z, value & 63, 0).astype(F32).astype(BF16)
    wanted = (dot(high, column) * 64.0 + dot(low, column)).astype(I32) - 1
    for dz in range(NZ):
        s1[dz] = jnp.broadcast_to(wanted[dz : dz + 1, :], (8, 128))
    k_c = dplane_c * NZ + dz_c
    k_r = dplane_r * NZ + dz_r
    pl.semaphore_wait(barrier, NZ - 1 + NPLANE - 1 + 1)

    for dz in range(1, NZ):
        send(s1.at[dz], r1.at[dz], ssem.at[0], rsem.at[0], (plane * NZ + z_up[dz], mp))
    r1[0] = s1[0]
    wait_bytes(r1.at[pl.ds(0, NZ - 1)], rsem.at[0])
    sub = iota((8, 128), 0)
    gathered = jnp.zeros((8, 128), I32)
    for dz in range(NZ):
        gathered = jnp.where(sub == dz, r1[dz], gathered)
    s2[...] = gathered
    for dp in range(1, NPLANE):
        send(s2, r2.at[dp], ssem.at[1], rsem.at[1], (peer(plane, z, dp, 0), mp))
    r2[0] = gathered
    wait_bytes(r2.at[pl.ds(0, NPLANE - 1)], rsem.at[1])

    table = r2[...].reshape(NG, 128)
    table_t = table.T
    lanes, subs = iota((NG, 128), 1), iota((NG, 128), 0)
    asked = []
    for j in range(CAP):
        asked.append(
            jnp.sum(jnp.where(lanes == (subs >> 3) * CAP + j, table, 0), axis=1, keepdims=True)
        )
        asked_ref[j : j + 1, :] = jnp.sum(
            jnp.where(subs == (lanes >> 3) * CAP + j, table_t, 0), axis=0, keepdims=True
        )

    loads[0].wait()
    loads[1].wait()
    for j in range(CAP):
        pick = onehot(asked[j] == iota((NG, ROWS), 1))
        part_k = dot(pick, kbuf[...])
        part_v = dot(pick, vbuf[...])
        for c in range(2):
            fst[pl.ds(4 * j + c, NG, stride=16), :] = part_k[:, c * 128 : (c + 1) * 128]
            fst[pl.ds(4 * j + 2 + c, NG, stride=16), :] = part_v[:, c * 128 : (c + 1) * 128]
    kv_send[...] = fst[...].reshape(NG, 16, 128).astype(BF16)

    @pl.loop(0, NPLANE)
    def _(dp):
        base = lax.rem(plane - dp + NPLANE, NPLANE) * NZ
        for dz in range(1, NZ):
            k = dp * NZ + dz
            send(kv_send.at[k], kv_recv.at[k], ssem.at[2], rsem.at[2], (base + z_down[dz], mp))

    @pl.loop(1, NPLANE)
    def _(dp):
        base = lax.rem(plane - dp + NPLANE, NPLANE) * NZ
        send(kv_send.at[dp * NZ], kv_recv.at[dp * NZ], ssem.at[2], rsem.at[2], (base + z, mp))

    kv_recv[0] = kv_send[0]

    for load in loads[2:]:
        load.wait()

    @pl.loop(0, ROWS // (2 * BLK))
    def _(step):
        for half in range(2):
            b = 2 * step + half
            rows = pl.ds(pl.multiple_of(b * BLK, BLK), BLK)
            qm = head_stack(qbuf[rows, :] * 0.125)
            gm = head_stack(gbuf[rows, :])
            s_own = dot(kbuf[rows, :], qm, NT)
            d_own = dot(vbuf[rows, :], gm, NT)
            top = jnp.max(s_own, 0, keepdims=True)
            p_own = jnp.exp2((s_own - top) * LOG2E)
            pbuf[rows, :] = p_own
            dbuf[rows, :] = d_own
            stats[b, 0:1, :] = top
            stats[b, 1:2, :] = jnp.sum(p_own, 0, keepdims=True)
            stats[b, 2:3, :] = jnp.sum(p_own * d_own, 0, keepdims=True)

    for j in range(CAP):
        pick = onehot(asked[j] == iota((NG, ROWS), 1))
        part_n = dot(pick, nbuf[...])
        for c in range(4):
            fst[pl.ds(4 * j + c, NG, stride=16), :] = part_n[:, c * 128 : (c + 1) * 128]
    n_send[...] = fst[...].reshape(NG, 16, 128).astype(BF16)
    gw[...] = jnp.zeros_like(gw)
    far_acc[...] = jnp.zeros_like(far_acc)

    wait_bytes(kv_recv.at[pl.ds(0, NG - 1)], rsem.at[2])
    fst[...] = kv_recv[...].astype(F32).reshape(NG * 16, 128)
    for j in range(CAP):
        for c in range(4):
            stack[j * NG : (j + 1) * NG, c * 128 : (c + 1) * 128] = fst[
                pl.ds(4 * j + c, NG, stride=16), :
            ].astype(BF16)
    place_mat = onehot(rank_c * NG + k_c == iota((HR, CAP * NG), 1))
    far_kv[...] = dot(place_mat, stack[...]).astype(BF16)
    far_kt[...] = (far_kv[:, 0:W] * 0.125).T

    mine_rows = pl.ds(pl.multiple_of(mp * W, W), W)
    other_rows = pl.ds(pl.multiple_of((1 - mp) * W, W), W)

    def attend(step):
        far_k = far_kv[:, 0:W]
        far_v = far_kv[:, W : 2 * W]
        slopes_far, lows_far, queries, grads = [], [], [], []
        for half in range(2):
            b = 2 * step + half
            rows = pl.ds(pl.multiple_of(b * BLK, BLK), BLK)
            qm = head_stack(qbuf[rows, :] * 0.125)
            gm = head_stack(gbuf[rows, :])
            bias = [jnp.where(pattern_ref[h, b] > 0, 0.0, 1e30).astype(F32) for h in range(2)]
            s_far = dot(far_k, qm, NT)
            d_far = dot(far_v, gm, NT)
            top_own = stats[b, 0:1, :]
            top = jnp.maximum(
                top_own,
                jnp.maximum(
                    jnp.max(s_far[0:BLK], 0, keepdims=True) - bias[0],
                    jnp.max(s_far[BLK:], 0, keepdims=True) - bias[1],
                ),
            )
            p_far = jnp.concatenate(
                [
                    jnp.exp2((s_far[0:BLK] - (top + bias[0])) * LOG2E),
                    jnp.exp2((s_far[BLK:] - (top + bias[1])) * LOG2E),
                ],
                0,
            )
            share = jnp.exp2((top_own - top) * LOG2E)
            inv = 1.0 / (stats[b, 1:2, :] * share + jnp.sum(p_far, 0, keepdims=True))
            term = (stats[b, 2:3, :] * share + jnp.sum(p_far * d_far, 0, keepdims=True)) * inv
            prob_own = pbuf[rows, :] * (share * inv)
            prob_far = p_far * inv
            slope_own = (prob_own * (dbuf[rows, :] - term)).astype(BF16)
            slope_far = (prob_far * (d_far - term)).astype(BF16)
            low_own = prob_own.astype(BF16)
            low_far = prob_far.astype(BF16)
            dk = dot(slope_own, qm)
            dv = dot(low_own, gm)
            kt = (kbuf[rows, :] * 0.125).T
            dqt = jnp.concatenate(
                [
                    dot(kt[h * E : (h + 1) * E, :], slope_own[:, h * BLK : (h + 1) * BLK])
                    + dot(far_kt[h * E : (h + 1) * E, :], slope_far[:, h * BLK : (h + 1) * BLK])
                    for h in range(HEADS_LOCAL)
                ],
                0,
            )
            grads.append((dqt.T.astype(BF16), dk.astype(BF16), dv.astype(BF16)))
            slopes_far.append(slope_far)
            lows_far.append(low_far)
            queries.append((qm, gm))

        far_acc[:, 0:W] += dot(
            jnp.concatenate(slopes_far, 1), jnp.concatenate([a for a, _ in queries], 0)
        )
        far_acc[:, W : 2 * W] += dot(
            jnp.concatenate(lows_far, 1), jnp.concatenate([a for _, a in queries], 0)
        )
        rows = pl.ds(pl.multiple_of(step * 2 * BLK, 2 * BLK), 2 * BLK)
        nodes = nbuf[rows, :]
        kept = jnp.zeros((2 * BLK, W), F32)
        given = jnp.zeros((2 * BLK, W), F32)
        for i in range(3):
            grad = jnp.concatenate([grads[0][i], grads[1][i]], 0)
            gw[:, i * W : (i + 1) * W] += dot(nodes, grad, TN)
            kept += dot(grad, wbuf[i, mine_rows, :], NT)
            given += dot(grad, wbuf[i, other_rows, :], NT)
        mine[rows, :] = kept
        e_send[rows, :] = given.astype(BF16)
        send(e_send.at[rows], e_recv.at[rows], ssem.at[6], rsem.at[6], twin)

    first_plane = mp * (NPLANE // 2)

    def send_nodes(i):
        dp = first_plane + i
        base = lax.rem(plane - dp + NPLANE, NPLANE) * NZ
        for dz in range(1, NZ):
            k = i * NZ + dz
            send(
                n_send.at[dp * NZ + dz], n_recv.at[k], ssem.at[3], rsem.at[3],
                (base + z_down[dz], mp),
            )

    @pl.loop(1, NPLANE // 2)
    def _(i):
        dp = first_plane + i
        base = lax.rem(plane - dp + NPLANE, NPLANE) * NZ
        send(n_send.at[dp * NZ], n_recv.at[i * NZ], ssem.at[3], rsem.at[3], (base + z, mp))

    @pl.when(mp == 1)
    def _():
        base = lax.rem(plane + NPLANE // 2, NPLANE) * NZ
        send(n_send.at[HALF], n_recv.at[0], ssem.at[4], rsem.at[4], (base + z, mp))

    @pl.when(mp == 0)
    def _():
        n_recv[0] = n_send[0]

    steps = ROWS // (2 * BLK)
    early = steps // 2

    @pl.loop(0, early)
    def _(step):
        send_nodes(2 * step)
        send_nodes(2 * step + 1)
        attend(step)

    k_ch = k_c - mp * HALF
    slot_c = jnp.where((k_ch >= 0) & (k_ch < HALF), rank_c * HALF + k_ch, -1)
    k_rh = k_r - mp * HALF
    slot_r = jnp.where((k_rh >= 0) & (k_rh < HALF), rank_r * HALF + k_rh, -1)
    wait_bytes(n_recv.at[pl.ds(0, HALF - 1)], rsem.at[3])

    @pl.when(mp == 1)
    def _():
        wait_bytes(n_recv.at[0], rsem.at[4])

    fst[0 : HALF * 16, :] = n_recv[...].astype(F32).reshape(HALF * 16, 128)
    for j in range(CAP):
        for c in range(4):
            stack[j * HALF : (j + 1) * HALF, c * 128 : (c + 1) * 128] = fst[
                pl.ds(4 * j + c, HALF, stride=16), :
            ].astype(BF16)
    place_half = onehot(slot_c == iota((HR, CAP * HALF), 1))
    fn_send[...] = dot(place_half, stack[0 : CAP * HALF, :]).astype(BF16)
    send(fn_send, fn_recv, ssem.at[5], rsem.at[5], twin)

    @pl.loop(early, steps)
    def _(step):
        attend(step)

    dk_far = far_acc[:, 0:W].astype(BF16)
    dv_far = far_acc[:, W : 2 * W].astype(BF16)
    t_send[...] = (dot(dk_far, wbuf[1], NT) + dot(dv_far, wbuf[2], NT)).astype(BF16)
    send(t_send, t_recv, ssem.at[7], rsem.at[7], twin)
    wait_bytes(fn_recv, rsem.at[5])
    far_nodes = fn_send[...] + fn_recv[...]
    gw[:, W : 2 * W] += dot(far_nodes, dk_far, TN)
    gw[:, 2 * W : 3 * W] += dot(far_nodes, dv_far, TN)
    y_send[...] = gw[...].astype(BF16).reshape(NY, 128, 3 * W)
    for d in range(1, NY):
        yy = lax.rem(y + d, NY)
        send(y_send.at[yy], y_recv.at[d - 1], ssem.at[8], rsem.at[8], ((yy * NX + x) * NZ + z, mp))

    place_t = onehot(slot_r == iota((CAP * HALF, HR), 0))
    wait_bytes(t_recv, rsem.at[7])
    summed = (t_send[...].astype(F32) + t_recv[...].astype(F32)).astype(BF16)
    placed = dot(place_t, summed)
    for j in range(CAP):
        for c in range(4):
            fst2[pl.ds(4 * j + c, HALF, stride=16), :] = placed[
                j * HALF : (j + 1) * HALF, c * 128 : (c + 1) * 128
            ]
    z_send[...] = fst2[...].reshape(HALF, 16, 128).astype(BF16)

    @pl.loop(0, NPLANE // 2)
    def _(i):
        base = lax.rem(plane + first_plane + i, NPLANE) * NZ
        for dz in range(1, NZ):
            k = i * NZ + dz
            send(z_send.at[k], z_recv.at[k], ssem.at[9], rsem.at[9], (base + z_up[dz], mp))

    @pl.loop(1, NPLANE // 2)
    def _(i):
        base = lax.rem(plane + first_plane + i, NPLANE) * NZ
        send(z_send.at[i * NZ], z_recv.at[i * NZ], ssem.at[9], rsem.at[9], (base + z, mp))

    @pl.when(mp == 1)
    def _():
        base = lax.rem(plane + NPLANE // 2, NPLANE) * NZ
        send(z_send.at[0], z_recv.at[0], ssem.at[10], rsem.at[10], (base + z, mp))

    @pl.when(mp == 0)
    def _():
        z_recv[0] = z_send[0]

    wait_bytes(y_recv, rsem.at[8])
    own = gw[pl.ds(pl.multiple_of(y * 128, 128), 128), :]
    for d in range(NY - 1):
        own += y_recv[d].astype(F32)
    gw[0:128, :] = own
    xx_send[...] = own.astype(BF16).reshape(NX, 32, 3 * W)
    for d in range(1, NX):
        xx = lax.rem(x + d, NX)
        send(xx_send.at[xx], xx_recv.at[d - 1], ssem.at[11], rsem.at[11], ((y * NX + xx) * NZ + z, mp))
    wait_bytes(xx_recv, rsem.at[11])
    own = gw[pl.ds(pl.multiple_of(x * 32, 32), 32), :]
    for d in range(NX - 1):
        own += xx_recv[d].astype(F32)
    for zz in range(NZ):
        for c in range(6):
            zz_send[zz, 4 * c : 4 * c + 4, :] = own[4 * zz : 4 * zz + 4, c * 128 : (c + 1) * 128]
    for d in range(1, NZ):
        send(
            zz_send.at[z_up[d]], zz_recv.at[d], ssem.at[12], rsem.at[12], (plane * NZ + z_up[d], mp)
        )
    zz_recv[0] = zz_send[z]

    wait_bytes(z_recv.at[pl.ds(0, HALF - 1)], rsem.at[9])

    @pl.when(mp == 1)
    def _():
        wait_bytes(z_recv.at[0], rsem.at[10])

    fst2[...] = z_recv[...].astype(F32).reshape(HALF * 16, 128)
    for j in range(CAP):
        for c in range(2):
            x_send[j, :, c * 128 : (c + 1) * 128] = fst2[
                pl.ds(4 * j + 2 * (1 - mp) + c, HALF, stride=16), :
            ].astype(BF16)
    send(x_send, z_full.at[:, mp], ssem.at[13], rsem.at[13], twin)
    for j in range(CAP):
        for c in range(2):
            z_full[j, mp, :, c * 128 : (c + 1) * 128] = fst2[
                pl.ds(4 * j + 2 * mp + c, HALF, stride=16), :
            ].astype(BF16)

    wait_bytes(zz_recv.at[pl.ds(0, NZ - 1)], rsem.at[12])
    final = zz_recv[0]
    for d in range(1, NZ):
        final += zz_recv[d]
    for r in range(4):
        for c in range(6):
            weights_out[r, c // 2 : c // 2 + 1, (c % 2) * 128 : (c % 2 + 1) * 128] = final[
                4 * c + r : 4 * c + r + 1, :
            ]

    wait_bytes(e_recv, rsem.at[6])
    wait_bytes(x_send, rsem.at[13])
    far = z_full[...].reshape(CAP * NG, W)
    chunk = 256

    @pl.loop(0, ROWS // chunk)
    def _(i):
        base = pl.multiple_of(i * chunk, chunk)
        row = iota((chunk, NG), 0) + base
        scatter = jnp.concatenate(
            [onehot(row == asked_ref[j : j + 1, :]) for j in range(CAP)], 1
        )
        rows = pl.ds(base, chunk)
        obuf[rows, :] = (
            mine[rows, :] + e_recv[rows, :].astype(F32) + dot(scatter, far)
        ).astype(BF16)
        pltpu.make_async_copy(obuf.at[rows], nodes_out.at[rows], osem).start()

    wait_bytes(s1.at[pl.ds(0, NZ - 1)], ssem.at[0])
    wait_bytes(r2.at[pl.ds(0, NPLANE - 1)], ssem.at[1])
    wait_bytes(kv_send.at[pl.ds(0, NG - 1)], ssem.at[2])
    wait_bytes(n_recv.at[pl.ds(0, HALF - 1)], ssem.at[3])
    wait_bytes(fn_recv, ssem.at[5])
    wait_bytes(e_recv, ssem.at[6])
    wait_bytes(t_recv, ssem.at[7])
    wait_bytes(y_recv, ssem.at[8])
    wait_bytes(z_recv.at[pl.ds(0, HALF - 1)], ssem.at[9])
    wait_bytes(xx_recv, ssem.at[11])
    wait_bytes(zz_recv.at[pl.ds(0, NZ - 1)], ssem.at[12])
    wait_bytes(x_send, ssem.at[13])

    @pl.when(mp == 1)
    def _():
        wait_bytes(n_recv.at[0], ssem.at[4])
        wait_bytes(z_recv.at[0], ssem.at[10])

    wait_bytes(obuf, osem)


VM = pl.BlockSpec(memory_space=pltpu.VMEM)
ANY = pl.BlockSpec(memory_space=pl.ANY)
LIMIT = 56 * 1024 * 1024


def on_device(
    nodes_in, query, keys, values, grad_attn, w_query, w_key, w_value, halo_owner, halo_row, pattern
):
    dma = pltpu.SemaphoreType.DMA
    vm = pltpu.VMEM
    return pl.pallas_call(
        layer_kernel,
        out_shape=(
            jax.ShapeDtypeStruct((ROWS, W), BF16),
            jax.ShapeDtypeStruct((4, 3, W), F32),
        ),
        in_specs=[pl.BlockSpec(memory_space=pltpu.SMEM), VM, VM] + [ANY] * 8,
        out_specs=(ANY, VM),
        scratch_shapes=[
            vm((ROWS, W), BF16),
            vm((ROWS, W), BF16),
            vm((ROWS, W), BF16),
            vm((ROWS, W), BF16),
            vm((ROWS, 2 * W), BF16),
            vm((3, 2 * W, W), BF16),
            vm((ROWS, W), BF16),
            vm((NZ, 8, 128), I32),
            vm((NZ, 8, 128), I32),
            vm((8, 128), I32),
            vm((NPLANE, 8, 128), I32),
            vm((NG * 16, 128), F32),
            vm((NG, 16, 128), BF16),
            vm((NG, 16, 128), BF16),
            vm((NG, 16, 128), BF16),
            vm((HALF, 16, 128), BF16),
            vm((CAP * NG, 2 * W), BF16),
            vm((HR, 2 * W), BF16),
            vm((HR, 2 * W), BF16),
            vm((8, 128), I32),
            vm((HR, 2 * W), BF16),
            vm((W, HR), BF16),
            vm((HR, 2 * W), F32),
            vm((ROWS, HEADS_LOCAL * BLK), F32),
            vm((ROWS, HEADS_LOCAL * BLK), F32),
            vm((ROWS // BLK, 8, HEADS_LOCAL * BLK), F32),
            vm((2 * W, 3 * W), F32),
            vm((ROWS, W), F32),
            vm((ROWS, W), BF16),
            vm((ROWS, W), BF16),
            vm((HR, 2 * W), BF16),
            vm((HR, 2 * W), BF16),
            vm((HALF * 16, 128), F32),
            vm((HALF, 16, 128), BF16),
            vm((HALF, 16, 128), BF16),
            vm((CAP, HALF, W), BF16),
            vm((CAP, 2, HALF, W), BF16),
            vm((NY, 128, 3 * W), BF16),
            vm((NY - 1, 128, 3 * W), BF16),
            vm((NX, 32, 3 * W), BF16),
            vm((NX - 1, 32, 3 * W), BF16),
            vm((NZ, 24, 128), F32),
            vm((NZ, 24, 128), F32),
            dma((8,)),
            dma,
            dma((14,)),
            dma((14,)),
        ],
        compiler_params=pltpu.CompilerParams(
            collective_id=0, has_side_effects=True, vmem_limit_bytes=LIMIT
        ),
        name="layer",
    )(
        pattern.T, halo_owner.reshape(1, HR), halo_row.reshape(1, HR),
        query, keys, values, grad_attn, nodes_in, w_query, w_key, w_value,
    )


def solution(mesh):
    in_specs = (
        P("graph", None),
        P("graph", "mp"),
        P("graph", "mp"),
        P("graph", "mp"),
        P("graph", "mp"),
        P(None, "mp"),
        P(None, "mp"),
        P(None, "mp"),
        P("graph", None),
        P("graph"),
        P("graph", None),
    )
    out_specs = (P("graph", "mp"), P("graph", None, "mp"))
    return jax.shard_map(
        on_device, mesh=mesh, in_specs=in_specs, out_specs=out_specs, check_vma=False
    )
```

time: 444 us -> 88.1 us (0.20); the launches traced: 437 us -> 87.5 us
  waiting for transfers between devices: 227 us -> 0 us
  Pallas kernels: 0 us -> 83.2 us
  local copies, waits for them, and re-layouts: 79.1 us -> 3.58 us
  matrix products: 44.5 us -> 0 us
  starting transfers between devices: 38.3 us -> 0 us
  other arithmetic: 31.4 us -> 0 us
  between operations: 16.8 us -> 0.64 us
    unnamed x3 -> x0, waiting for transfers between devices: 219 us -> none
    pallas_call x0 -> x1, Pallas kernels: none -> 83.2 us  [on_device(): pl.pallas_call(layer_kernel, out_shape=(jax.ShapeDtypeStruct((ROWS, W), B...]
    dot_general x12 -> x0, matrix products: 44.5 us -> none  [the longest x1 6.83 us: attend_blocks(): jnp.einsum('bhqk,bqhe->khe', low_far, douts_b, preferred_element_type=wide)]
    reshape x14 -> x0, local copies, waits for them, and re-layouts: 41.7 us -> none  [the longest x2 10.3 us: on_device(): grad_k_own.reshape(rows_dev, width_local) + added[:, :width_local]]
    all_to_all x3 -> x0, starting transfers between devices: 38.2 us -> none  [the longest x1 15.4 us: on_device(): lax.all_to_all(wanted, 'graph', split_axis=0, concat_axis=0, tiled=True)]
    unnamed x52 -> x1, local copies, waits for them, and re-layouts: 13.8 us -> 2.26 us
    convert_element_type x4 -> x0, other arithmetic: 11.4 us -> none  [the longest x1 3.99 us: on_device(): (grad_k_own.reshape(rows_dev, width_local) + added[:, :width_local]).asty...]
    convert_element_type x3 -> x0, local copies, waits for them, and re-layouts: 10.4 us -> none  [the longest x2 8.42 us: on_device(): grad_query = grad_q.reshape(rows_dev, width_local).astype(jnp.bfloat16)]
  transfers between devices with their start and end apart: 5 -> 0, of which waited for: 2 -> 0; matrix products, arithmetic and copies ran while one was open for 15% -> 0% of each run, Pallas kernels for 0% -> 0%
where the time goes in v2:
time: 88.1 us; the launch traced here: 87.5 us
  Pallas kernels  83.2 us (94%)
  local copies, waits for them, and re-layouts  3.58 us (4%)
    pallas_call x1, Pallas kernels, on_device(): pl.pallas_call(layer_kernel, out_shape=(jax.ShapeDtypeStruct((ROWS, W), B...  83.2 us
    unnamed x1, local copies, waits for them, and re-layouts  2.26 us

profile of v2, /device:TPU:2, one launch (start us, length us, event | category | flops | bytes accessed | tf_op | source)
XLA Modules:
  0.0 87.5 jit_solution(13700433268563060879)
XLA Ops:
  0.6 83.2 %layer.1 = (bf16[2048,256]{1,0:T(8,128)(2,1)}, f32[4,3,256]{2,1,0:T(4,128)}) custom-call(s32[2,16]{1,0:T(2,128)} %bitcast.3, s32[1,256]{1,0:T(1,128)} %bitcast.4, s32[1,256]{1,0:T(1,128)} %bitcast.5, bf16[2048,256]{1,0:T(8,128)(2,1)} %query_hbm.1, bf16[2048,256]{1,0:T(8,128)(2,1)} %keys_hbm.1, bf16[2048,256]{1,0:T(8,128)(2,1)} %values_hbm.1, ...), custom_call_target="tpu_custom_call" | custom-call | tf_op jit(solution)/shard_map/layer/pallas_call | solution.py:516
  83.9 1.3 %copy.13 = f32[4,3,256]{2,0,1:T(4,128)} copy(f32[4,3,256]{2,1,0:T(4,128)} %get-tuple-element.3) | data formatting | bytes 24576 | tf_op jit(solution)/shard_map/layer/pallas_call | solution.py:516
  85.2 2.3 %copy.15 = bf16[2048,256]{1,0:T(8,128)(2,1)} copy(bf16[2048,256]{1,0:T(8,128)(2,1)} %get-tuple-element.6) | data formatting | bytes 2097152

commit v3 on v2

v3 whole, which is shorter than its diff:
```python
import functools
import math

import jax
import jax.numpy as jnp
from jax import lax
from jax.experimental import pallas as pl
from jax.experimental.pallas import tpu as pltpu
from jax.sharding import PartitionSpec as P

MESH = pl.DeviceIdType.MESH
F32 = jnp.float32
BF16 = jnp.bfloat16
I32 = jnp.int32

HEADS_LOCAL = 4
E = 64
BLK = 128
ROWS = 2048
W = 256
HR = 256
CAP = 4
NX, NY, NZ = 4, 4, 8
NG = NX * NY * NZ
NPLANE = NX * NY
HALF = NG // 2
LOG2E = 1.4426950408889634
NT = (((1,), (1,)), ((), ()))
TN = (((0,), (0,)), ((), ()))


def dot(a, b, dims=(((1,), (0,)), ((), ()))):
    return lax.dot_general(a, b, dims, preferred_element_type=F32)


def iota(shape, dim):
    return lax.broadcasted_iota(I32, shape, dim)


def place():
    me = lax.axis_index("graph")
    mp = lax.axis_index("mp")
    return me, mp, lax.div(me, NZ), lax.rem(me, NZ)


def peer(plane, z, dplane, dz):
    return lax.rem(plane + dplane, NPLANE) * NZ + lax.rem(z + dz, NZ)


def relative(owner, plane, z):
    dplane = ((owner >> 3) - plane + NPLANE) & (NPLANE - 1)
    dz = ((owner & 7) - z + NZ) & (NZ - 1)
    return dplane, dz


def rank_column(owner_c, owner_r):
    same = (owner_c == owner_r) & (iota((HR, HR), 1) < iota((HR, HR), 0))
    return jnp.sum(jnp.where(same, 1, 0), axis=1, keepdims=True)


def rank_row(owner_c, owner_r):
    same = (owner_c == owner_r) & (iota((HR, HR), 0) < iota((HR, HR), 1))
    return jnp.sum(jnp.where(same, 1, 0), axis=0, keepdims=True)


def onehot(mask):
    return jnp.where(mask, 1.0, 0.0).astype(BF16)


def wait_bytes(ref, sem):
    pltpu.make_async_copy(ref, ref, sem).wait()


def send(src, dst, ssem, rsem, dev):
    pltpu.make_async_remote_copy(
        src_ref=src, dst_ref=dst, send_sem=ssem, recv_sem=rsem, device_id=dev, device_id_type=MESH
    ).start()


def head_stack(x):
    head_of_lane = iota((2 * BLK, W), 1) // E
    return jnp.concatenate(
        [jnp.where(head_of_lane == h, x, 0.0).astype(BF16) for h in range(HEADS_LOCAL)], 0
    )


def block_rows(x, half):
    return jnp.concatenate(
        [x[(2 * h + half) * BLK : (2 * h + half + 1) * BLK, :] for h in range(HEADS_LOCAL)], 0
    )


def block_lanes(x, half):
    return jnp.concatenate(
        [x[:, (2 * h + half) * BLK : (2 * h + half + 1) * BLK] for h in range(HEADS_LOCAL)], 1
    )


def layer_kernel(
    pattern_hbm, owner_hbm, row_hbm,
    query_hbm, keys_hbm, values_hbm, grad_hbm, nodes_hbm, wq_hbm, wk_hbm, wv_hbm,
    nodes_out, weights_out,
    qbuf, kbuf, vbuf, gbuf, nbuf, wbuf,
    s1, r1, s2, r2, fst, kv_send, kv_recv, n_send, n_recv, stack, fn_send, fn_recv,
    pattern_ref, owner_ref, row_ref, asked_ref, far_kv, far_kt, far_acc, pbuf, dbuf, stats, gw, mine, e_recv,
    qms, gms, kts, ntr, scat, grads, even, odd,
    t_recv, z_send, z_recv, x_send, z_full,
    a_send, a_recv, b_send, b_recv, a_sum, b_sum, a2_send, a2_recv, b2_send, b2_recv,
    zz_send, zz_recv,
    lsem, ssem, rsem,
):
    me, mp, plane, z = place()
    y, x = lax.div(plane, NX), lax.rem(plane, NX)
    twin = (me, 1 - mp)
    loads = [
        pltpu.make_async_copy(src, dst, lsem.at[i])
        for i, (src, dst) in enumerate(
            (
                (keys_hbm, kbuf),
                (values_hbm, vbuf),
                (query_hbm, qbuf),
                (grad_hbm, gbuf),
                (nodes_hbm, nbuf),
                (wq_hbm, wbuf.at[0]),
                (wk_hbm, wbuf.at[1]),
                (wv_hbm, wbuf.at[2]),
                (owner_hbm, owner_ref),
                (row_hbm, row_ref),
                (pattern_hbm, pattern_ref),
            )
        )
    ]
    z_up = [lax.rem(z + d, NZ) for d in range(NZ)]
    z_down = [lax.rem(z - d + NZ, NZ) for d in range(NZ)]

    barrier = pltpu.get_barrier_semaphore()
    for d in range(1, NZ):
        pl.semaphore_signal(barrier, inc=1, device_id=(plane * NZ + z_up[d], mp), device_id_type=MESH)
    for d in range(1, NPLANE):
        pl.semaphore_signal(barrier, inc=1, device_id=(peer(plane, z, d, 0), mp), device_id_type=MESH)
    pl.semaphore_signal(barrier, inc=1, device_id=twin, device_id_type=MESH)

    for load in loads[8:] + loads[0:2]:
        load.start()

    for load in loads[8:]:
        load.wait()
    owner_r, row_r = owner_ref[...], row_ref[...]
    owner_c = jnp.broadcast_to(owner_r, (HR, HR)).T
    rank_c = rank_column(owner_c, owner_r)
    rank_r = rank_row(owner_c, owner_r)
    dplane_c, dz_c = relative(owner_c[:, 0:1], plane, z)
    dplane_r, dz_r = relative(owner_r, plane, z)
    column = onehot(dplane_c * CAP + rank_c == iota((HR, 128), 1))
    value = row_r + 1
    at_z = dz_r == iota((NZ, HR), 0)
    high = jnp.where(at_z, value >> 6, 0).astype(F32).astype(BF16)
    low = jnp.where(at_z, value & 63, 0).astype(F32).astype(BF16)
    wanted = (dot(high, column) * 64.0 + dot(low, column)).astype(I32) - 1
    for dz in range(NZ):
        s1[dz] = wanted[dz : dz + 1, :]
    k_c = dplane_c * NZ + dz_c
    k_r = dplane_r * NZ + dz_r
    pl.semaphore_wait(barrier, NZ - 1 + NPLANE - 1 + 1)

    for dz in range(1, NZ):
        send(s1.at[dz], r1.at[dz], ssem.at[0], rsem.at[0], (plane * NZ + z_up[dz], mp))
    r1[0] = s1[0]
    wait_bytes(r1.at[pl.ds(0, NZ - 1)], rsem.at[0])
    sub = iota((8, 128), 0)
    gathered = jnp.zeros((8, 128), I32)
    for dz in range(NZ):
        gathered = jnp.where(sub == dz, r1[dz], gathered)
    s2[...] = gathered
    for dp in range(1, NPLANE):
        send(s2, r2.at[dp], ssem.at[1], rsem.at[1], (peer(plane, z, dp, 0), mp))
    r2[0] = gathered
    wait_bytes(r2.at[pl.ds(0, NPLANE - 1)], rsem.at[1])

    for load in loads[2:8]:
        load.start()
    table = r2[...].reshape(NG, 128)
    table_t = table.T
    lanes, subs = iota((NG, 128), 1), iota((NG, 128), 0)
    asked = []
    for j in range(CAP):
        asked.append(
            jnp.sum(jnp.where(lanes == (subs >> 3) * CAP + j, table, 0), axis=1, keepdims=True)
        )
        asked_ref[j : j + 1, :] = jnp.sum(
            jnp.where(subs == (lanes >> 3) * CAP + j, table_t, 0), axis=0, keepdims=True
        )

    loads[0].wait()
    loads[1].wait()
    for j in range(CAP):
        pick = onehot(asked[j] == iota((NG, ROWS), 1))
        part_k = dot(pick, kbuf[...])
        part_v = dot(pick, vbuf[...])
        for c in range(2):
            fst[pl.ds(4 * j + c, NG, stride=16), :] = part_k[:, c * 128 : (c + 1) * 128]
            fst[pl.ds(4 * j + 2 + c, NG, stride=16), :] = part_v[:, c * 128 : (c + 1) * 128]
    kv_send[...] = fst[...].reshape(NG, 16, 128).astype(BF16)

    @pl.loop(0, NPLANE)
    def _(dp):
        base = lax.rem(plane - dp + NPLANE, NPLANE) * NZ
        for dz in range(1, NZ):
            k = dp * NZ + dz
            send(kv_send.at[k], kv_recv.at[k], ssem.at[2], rsem.at[2], (base + z_down[dz], mp))

    @pl.loop(1, NPLANE)
    def _(dp):
        base = lax.rem(plane - dp + NPLANE, NPLANE) * NZ
        send(kv_send.at[dp * NZ], kv_recv.at[dp * NZ], ssem.at[2], rsem.at[2], (base + z, mp))

    kv_recv[0] = kv_send[0]

    for load in loads[2:8]:
        load.wait()

    @pl.loop(0, ROWS // (2 * BLK))
    def _(step):
        both = pl.ds(pl.multiple_of(step * 2 * BLK, 2 * BLK), 2 * BLK)
        qm = head_stack(qbuf[both, :] * 0.125)
        gm = head_stack(gbuf[both, :])
        qms[step] = qm
        gms[step] = gm
        kts[step] = (kbuf[both, :] * 0.125).T
        ntr[step] = nbuf[both, :].T
        for half in range(2):
            rows = pl.ds(pl.multiple_of(step * 2 * BLK + half * BLK, BLK), BLK)
            s_own = dot(kbuf[rows, :], block_rows(qm, half), NT)
            d_own = dot(vbuf[rows, :], block_rows(gm, half), NT)
            top = jnp.max(s_own, 0, keepdims=True)
            p_own = jnp.exp2((s_own - top) * LOG2E)
            total = jnp.sum(p_own, 0, keepdims=True)
            term = jnp.sum(p_own * d_own, 0, keepdims=True)
            for h in range(HEADS_LOCAL):
                src = slice(h * BLK, (h + 1) * BLK)
                dst = slice((2 * h + half) * BLK, (2 * h + half + 1) * BLK)
                pbuf[step, :, dst] = p_own[:, src]
                dbuf[step, :, dst] = d_own[:, src]
                stats[step, 0:1, dst] = top[:, src]
                stats[step, 1:2, dst] = total[:, src]
                stats[step, 2:3, dst] = term[:, src]

    for j in range(CAP):
        pick = onehot(asked[j] == iota((NG, ROWS), 1))
        part_n = dot(pick, nbuf[...])
        for c in range(4):
            fst[pl.ds(4 * j + c, NG, stride=16), :] = part_n[:, c * 128 : (c + 1) * 128]
    n_send[...] = fst[...].reshape(NG, 16, 128).astype(BF16)
    far_acc[...] = jnp.zeros_like(far_acc)
    odd[...] = jnp.zeros_like(odd)

    @pl.loop(0, ROWS // 256)
    def _(i):
        base = pl.multiple_of(i * 256, 256)
        row = iota((256, NG), 0) + base
        for j in range(CAP):
            scat[pl.ds(base, 256), j * NG : (j + 1) * NG] = onehot(row == asked_ref[j : j + 1, :])


    wait_bytes(kv_recv.at[pl.ds(0, NG - 1)], rsem.at[2])
    fst[...] = kv_recv[...].astype(F32).reshape(NG * 16, 128)
    for j in range(CAP):
        for c in range(4):
            stack[j * NG : (j + 1) * NG, c * 128 : (c + 1) * 128] = fst[
                pl.ds(4 * j + c, NG, stride=16), :
            ].astype(BF16)
    place_mat = onehot(rank_c * NG + k_c == iota((HR, CAP * NG), 1))
    far_kv[...] = dot(place_mat, stack[...]).astype(BF16)
    far_kt[...] = (far_kv[:, 0:W] * 0.125).T

    mine_rows = pl.ds(pl.multiple_of(mp * W, W), W)
    other_rows = pl.ds(pl.multiple_of((1 - mp) * W, W), W)

    def scores(step, h):
        rows = slice(2 * h * BLK, 2 * (h + 1) * BLK)
        return (
            dot(far_kv[:, 0:W], qms[step, rows, :], NT),
            dot(far_kv[:, W : 2 * W], gms[step, rows, :], NT),
        )

    def soften(step, h, bias, s_far, d_far, buf):
        lanes = slice(2 * h * BLK, 2 * (h + 1) * BLK)
        top_own = stats[step, 0:1, lanes]
        top = jnp.maximum(
            top_own,
            jnp.maximum(
                jnp.max(s_far[0:BLK], 0, keepdims=True) - bias[0],
                jnp.max(s_far[BLK:], 0, keepdims=True) - bias[1],
            ),
        )
        p_far = jnp.concatenate(
            [
                jnp.exp2((s_far[0:BLK] - (top + bias[0])) * LOG2E),
                jnp.exp2((s_far[BLK:] - (top + bias[1])) * LOG2E),
            ],
            0,
        )
        share = jnp.exp2((top_own - top) * LOG2E)
        inv = 1.0 / (stats[step, 1:2, lanes] * share + jnp.sum(p_far, 0, keepdims=True))
        term = (stats[step, 2:3, lanes] * share + jnp.sum(p_far * d_far, 0, keepdims=True)) * inv
        prob_own = pbuf[step, :, lanes] * (share * inv)
        prob_far = p_far * inv
        buf[0, 0:BLK, lanes] = (prob_own * (dbuf[step, :, lanes] - term)).astype(BF16)
        buf[0, BLK:, lanes] = (prob_far * (d_far - term)).astype(BF16)
        buf[1, 0:BLK, lanes] = prob_own.astype(BF16)
        buf[1, BLK:, lanes] = prob_far.astype(BF16)

    def apply(step, buf, part):
        first = pl.multiple_of(step * 2 * BLK, 2 * BLK)
        if part < 2:
            stacked = (qms, gms)[part]
            far_acc[:, part * W : (part + 1) * W] += dot(buf[part, BLK:, :], stacked[step])
        elif part == 2:
            pieces = []
            for h in range(HEADS_LOCAL):
                heads = slice(h * E, (h + 1) * E)
                own_part = [
                    dot(
                        kts[step, heads, half * BLK : (half + 1) * BLK],
                        buf[0, 0:BLK, (2 * h + half) * BLK : (2 * h + half + 1) * BLK],
                    )
                    for half in range(2)
                ]
                pieces.append(
                    dot(far_kt[heads, :], buf[0, BLK:, 2 * h * BLK : 2 * (h + 1) * BLK])
                    + jnp.concatenate(own_part, 1)
                )
            grads[pl.ds(first, 2 * BLK), 0:W] = jnp.concatenate(pieces, 0).T.astype(BF16)
        else:
            for i, stacked in enumerate((qms, gms)):
                for half in range(2):
                    rows = pl.ds(pl.multiple_of(first + half * BLK, BLK), BLK)
                    grads[rows, (i + 1) * W : (i + 2) * W] = dot(
                        block_lanes(buf[i, 0:BLK, :], half), block_rows(stacked[step], half)
                    ).astype(BF16)

    def attend(step, buf, before, buf_before):
        second = ((iota((1, 2 * BLK), 1) >> 7) & 1) == 1
        bias = []
        for h in range(2):
            each = [
                jnp.where(pattern_ref[h, 2 * step + half] > 0, 0.0, 1e30).astype(F32)
                for half in range(2)
            ]
            bias.append(jnp.where(second, each[1], each[0]))
        ready = scores(step, 0)
        for h in range(HEADS_LOCAL):
            now = ready
            if h + 1 < HEADS_LOCAL:
                ready = scores(step, h + 1)
            apply(before, buf_before, h)
            soften(step, h, bias, now[0], now[1], buf)

    def attend_pair(t):
        attend(2 * t, even, jnp.maximum(2 * t - 1, 0), odd)
        attend(2 * t + 1, odd, 2 * t, even)

    def project(step):
        both = pl.ds(pl.multiple_of(step * 2 * BLK, 2 * BLK), 2 * BLK)
        kept = jnp.zeros((2 * BLK, W), F32)
        given = jnp.zeros((2 * BLK, W), F32)
        for i in range(3):
            grad = grads[both, i * W : (i + 1) * W]
            kept += dot(grad, wbuf[i, mine_rows, :], NT)
            given += dot(grad, wbuf[i, other_rows, :], NT)
        mine[both, :] = kept
        gbuf[both, :] = given.astype(BF16)
        send(gbuf.at[both], e_recv.at[both], ssem.at[6], rsem.at[6], twin)

    first_plane = mp * (NPLANE // 2)

    @pl.loop(0, NPLANE // 2)
    def _(i):
        dp = first_plane + i
        base = lax.rem(plane - dp + NPLANE, NPLANE) * NZ
        for dz in range(1, NZ):
            send(
                n_send.at[dp * NZ + dz], n_recv.at[i * NZ + dz], ssem.at[3], rsem.at[3],
                (base + z_down[dz], mp),
            )

    @pl.loop(1, NPLANE // 2)
    def _(i):
        dp = first_plane + i
        base = lax.rem(plane - dp + NPLANE, NPLANE) * NZ
        send(n_send.at[dp * NZ], n_recv.at[i * NZ], ssem.at[3], rsem.at[3], (base + z, mp))

    @pl.when(mp == 1)
    def _():
        base = lax.rem(plane + NPLANE // 2, NPLANE) * NZ
        send(n_send.at[HALF], n_recv.at[0], ssem.at[4], rsem.at[4], (base + z, mp))

    @pl.when(mp == 0)
    def _():
        n_recv[0] = n_send[0]

    steps = ROWS // (2 * BLK)
    early = steps - 2

    @pl.loop(0, early // 2)
    def _(t):
        attend_pair(t)

    k_ch = k_c - mp * HALF
    slot_c = jnp.where((k_ch >= 0) & (k_ch < HALF), rank_c * HALF + k_ch, -1)
    k_rh = k_r - mp * HALF
    slot_r = jnp.where((k_rh >= 0) & (k_rh < HALF), rank_r * HALF + k_rh, -1)
    wait_bytes(n_recv.at[pl.ds(0, HALF - 1)], rsem.at[3])

    @pl.when(mp == 1)
    def _():
        wait_bytes(n_recv.at[0], rsem.at[4])

    fst[0 : HALF * 16, :] = n_recv[...].astype(F32).reshape(HALF * 16, 128)
    for j in range(CAP):
        for c in range(4):
            stack[j * HALF : (j + 1) * HALF, c * 128 : (c + 1) * 128] = fst[
                pl.ds(4 * j + c, HALF, stride=16), :
            ].astype(BF16)
    place_half = onehot(slot_c == iota((HR, CAP * HALF), 1))
    fn_send[...] = dot(place_half, stack[0 : CAP * HALF, :]).astype(BF16)
    send(fn_send, fn_recv, ssem.at[5], rsem.at[5], twin)

    @pl.loop(early // 2, steps // 2)
    def _(t):
        attend_pair(t)

    for part in range(4):
        apply(steps - 1, odd, part)

    dk_far = far_acc[:, 0:W].astype(BF16)
    dv_far = far_acc[:, W : 2 * W].astype(BF16)
    far_kv[...] = (dot(dk_far, wbuf[1], NT) + dot(dv_far, wbuf[2], NT)).astype(BF16)
    send(far_kv, t_recv, ssem.at[7], rsem.at[7], twin)
    wait_bytes(fn_recv, rsem.at[5])
    far_nodes = fn_send[...] + fn_recv[...]

    edge = 3 * W // 2
    for i in range(3):
        columns = slice(i * W, (i + 1) * W)
        part = jnp.zeros((2 * W, W), F32)
        for step in range(steps):
            part += dot(ntr[step], grads[step * 2 * BLK : (step + 1) * 2 * BLK, columns])
        if i == 1:
            part += dot(far_nodes, dk_far, TN)
        if i == 2:
            part += dot(far_nodes, dv_far, TN)
        gw[:, columns] = part
    a_send[...] = gw[:, 0:edge].astype(BF16).reshape(NY, 128, edge)
    for d in range(1, NY):
        yy = lax.rem(y + d, NY)
        send(a_send.at[yy], a_recv.at[d - 1], ssem.at[8], rsem.at[8], ((yy * NX + x) * NZ + z, mp))
    for yy in range(NY):
        for xx in range(NX):
            first = yy * 128 + xx * 32
            b_send[xx, yy] = gw[first : first + 32, edge:].astype(BF16)
    for d in range(1, NX):
        xx = lax.rem(x + d, NX)
        send(b_send.at[xx], b_recv.at[d - 1], ssem.at[14], rsem.at[14], ((y * NX + xx) * NZ + z, mp))

    place_t = onehot(slot_r == iota((CAP * HALF, HR), 0))
    wait_bytes(t_recv, rsem.at[7])
    summed = (far_kv[...].astype(F32) + t_recv[...].astype(F32)).astype(BF16)
    placed = dot(place_t, summed)
    for j in range(CAP):
        for c in range(4):
            fst[pl.ds(4 * j + c, HALF, stride=16), :] = placed[
                j * HALF : (j + 1) * HALF, c * 128 : (c + 1) * 128
            ]
    z_send[...] = fst[0 : HALF * 16, :].reshape(HALF, 16, 128).astype(BF16)

    @pl.loop(0, NPLANE // 2)
    def _(i):
        base = lax.rem(plane + first_plane + i, NPLANE) * NZ
        for dz in range(1, NZ):
            k = i * NZ + dz
            send(z_send.at[k], z_recv.at[k], ssem.at[9], rsem.at[9], (base + z_up[dz], mp))

    @pl.loop(1, NPLANE // 2)
    def _(i):
        base = lax.rem(plane + first_plane + i, NPLANE) * NZ
        send(z_send.at[i * NZ], z_recv.at[i * NZ], ssem.at[9], rsem.at[9], (base + z, mp))

    @pl.when(mp == 1)
    def _():
        base = lax.rem(plane + NPLANE // 2, NPLANE) * NZ
        send(z_send.at[0], z_recv.at[0], ssem.at[10], rsem.at[10], (base + z, mp))

    @pl.when(mp == 0)
    def _():
        z_recv[0] = z_send[0]

    @pl.loop(0, 4)
    def _(step):
        project(step)

    @pl.loop(4, steps)
    def _(step):
        project(step)

    wait_bytes(a_recv, rsem.at[8])
    own = gw[pl.ds(pl.multiple_of(y * 128, 128), 128), 0:edge]
    for d in range(NY - 1):
        own += a_recv[d].astype(F32)
    a_sum[...] = own
    a2_send[...] = own.astype(BF16).reshape(NX, 32, edge)
    for d in range(1, NX):
        xx = lax.rem(x + d, NX)
        send(a2_send.at[xx], a2_recv.at[d - 1], ssem.at[11], rsem.at[11], ((y * NX + xx) * NZ + z, mp))
    wait_bytes(b_recv, rsem.at[14])
    for yy in range(NY):
        own = gw[pl.ds(pl.multiple_of(yy * 128 + x * 32, 32), 32), edge:]
        for d in range(NX - 1):
            own += b_recv[d, yy].astype(F32)
        b_sum[yy * 32 : (yy + 1) * 32, :] = own
        b2_send[yy] = own.astype(BF16)
    for d in range(1, NY):
        yy = lax.rem(y + d, NY)
        send(b2_send.at[yy], b2_recv.at[d - 1], ssem.at[15], rsem.at[15], ((yy * NX + x) * NZ + z, mp))

    wait_bytes(a2_recv, rsem.at[11])
    wait_bytes(b2_recv, rsem.at[15])
    own_a = a_sum[pl.ds(pl.multiple_of(x * 32, 32), 32), :]
    own_b = b_sum[pl.ds(pl.multiple_of(y * 32, 32), 32), :]
    for d in range(NX - 1):
        own_a += a2_recv[d].astype(F32)
        own_b += b2_recv[d].astype(F32)
    for zz in range(NZ):
        for c in range(3):
            zz_send[zz, 4 * c : 4 * c + 4, :] = own_a[4 * zz : 4 * zz + 4, c * 128 : (c + 1) * 128]
            zz_send[zz, 4 * c + 12 : 4 * c + 16, :] = own_b[
                4 * zz : 4 * zz + 4, c * 128 : (c + 1) * 128
            ]
    for d in range(1, NZ):
        send(
            zz_send.at[z_up[d]], zz_recv.at[d], ssem.at[12], rsem.at[12], (plane * NZ + z_up[d], mp)
        )
    zz_recv[0] = zz_send[z]

    wait_bytes(z_recv.at[pl.ds(0, HALF - 1)], rsem.at[9])

    @pl.when(mp == 1)
    def _():
        wait_bytes(z_recv.at[0], rsem.at[10])

    fst[0 : HALF * 16, :] = z_recv[...].astype(F32).reshape(HALF * 16, 128)
    for j in range(CAP):
        for c in range(2):
            x_send[j, :, c * 128 : (c + 1) * 128] = fst[
                pl.ds(4 * j + 2 * (1 - mp) + c, HALF, stride=16), :
            ].astype(BF16)
    send(x_send, z_full.at[:, mp], ssem.at[13], rsem.at[13], twin)
    for j in range(CAP):
        for c in range(2):
            z_full[j, mp, :, c * 128 : (c + 1) * 128] = fst[
                pl.ds(4 * j + 2 * mp + c, HALF, stride=16), :
            ].astype(BF16)
    wait_bytes(e_recv, rsem.at[6])
    mine[...] += e_recv[...].astype(F32)

    wait_bytes(x_send, rsem.at[13])
    far = z_full[...].reshape(CAP * NG, W)

    @pl.loop(0, ROWS // 512)
    def _(i):
        rows = pl.ds(pl.multiple_of(i * 512, 512), 512)
        nodes_out[rows, :] = (mine[rows, :] + dot(scat[rows, :], far)).astype(BF16)

    wait_bytes(zz_recv.at[pl.ds(0, NZ - 1)], rsem.at[12])
    final = zz_recv[0]
    for d in range(1, NZ):
        final += zz_recv[d]
    for c in range(6):
        weights_out[c // 2, :, (c % 2) * 128 : (c % 2 + 1) * 128] = final[4 * c : 4 * c + 4, :]

    wait_bytes(s1.at[pl.ds(0, NZ - 1)], ssem.at[0])
    wait_bytes(r2.at[pl.ds(0, NPLANE - 1)], ssem.at[1])
    wait_bytes(kv_send.at[pl.ds(0, NG - 1)], ssem.at[2])
    wait_bytes(n_recv.at[pl.ds(0, HALF - 1)], ssem.at[3])
    wait_bytes(fn_recv, ssem.at[5])
    wait_bytes(e_recv, ssem.at[6])
    wait_bytes(t_recv, ssem.at[7])
    wait_bytes(a_recv, ssem.at[8])
    wait_bytes(b_recv, ssem.at[14])
    wait_bytes(z_recv.at[pl.ds(0, HALF - 1)], ssem.at[9])
    wait_bytes(a2_recv, ssem.at[11])
    wait_bytes(b2_recv, ssem.at[15])
    wait_bytes(zz_recv.at[pl.ds(0, NZ - 1)], ssem.at[12])
    wait_bytes(x_send, ssem.at[13])

    @pl.when(mp == 1)
    def _():
        wait_bytes(n_recv.at[0], ssem.at[4])
        wait_bytes(z_recv.at[0], ssem.at[10])


VM = pl.BlockSpec(memory_space=pltpu.VMEM)
HBM = pl.BlockSpec(memory_space=pltpu.HBM)
LIMIT = 56 * 1024 * 1024


def on_device(
    nodes_in, query, keys, values, grad_attn, w_query, w_key, w_value, halo_owner, halo_row, pattern
):
    dma = pltpu.SemaphoreType.DMA
    vm = pltpu.VMEM
    grad_nodes, grad_weights = pl.pallas_call(
        layer_kernel,
        out_shape=(
            jax.ShapeDtypeStruct((ROWS, W), BF16),
            jax.ShapeDtypeStruct((3, 4, W), F32),
        ),
        in_specs=[HBM] * 11,
        out_specs=(VM, VM),
        scratch_shapes=[
            vm((ROWS, W), BF16),
            vm((ROWS, W), BF16),
            vm((ROWS, W), BF16),
            vm((ROWS, W), BF16),
            vm((ROWS, 2 * W), BF16),
            vm((3, 2 * W, W), BF16),
            vm((NZ, 1, 128), I32),
            vm((NZ, 1, 128), I32),
            vm((8, 128), I32),
            vm((NPLANE, 8, 128), I32),
            vm((NG * 16, 128), F32),
            vm((NG, 16, 128), BF16),
            vm((NG, 16, 128), BF16),
            vm((NG, 16, 128), BF16),
            vm((HALF, 16, 128), BF16),
            vm((CAP * NG, 2 * W), BF16),
            vm((HR, 2 * W), BF16),
            vm((HR, 2 * W), BF16),
            pltpu.SMEM((2, ROWS // BLK), I32),
            vm((1, HR), I32),
            vm((1, HR), I32),
            vm((8, 128), I32),
            vm((HR, 2 * W), BF16),
            vm((W, HR), BF16),
            vm((HR, 2 * W), F32),
            vm((ROWS // 256, BLK, 8 * BLK), F32),
            vm((ROWS // 256, BLK, 8 * BLK), F32),
            vm((ROWS // 256, 8, 8 * BLK), F32),
            vm((2 * W, 3 * W), F32),
            vm((ROWS, W), F32),
            vm((ROWS, W), BF16),
            vm((ROWS // 256, 8 * BLK, W), BF16),
            vm((ROWS // 256, 8 * BLK, W), BF16),
            vm((ROWS // 256, W, 2 * BLK), BF16),
            vm((ROWS // 256, 2 * W, 2 * BLK), BF16),
            vm((ROWS, CAP * NG), BF16),
            vm((ROWS, 3 * W), BF16),
            vm((2, 3 * BLK, 8 * BLK), BF16),
            vm((2, 3 * BLK, 8 * BLK), BF16),
            vm((HR, 2 * W), BF16),
            vm((HALF, 16, 128), BF16),
            vm((HALF, 16, 128), BF16),
            vm((CAP, HALF, W), BF16),
            vm((CAP, 2, HALF, W), BF16),
            vm((NY, 128, 3 * W // 2), BF16),
            vm((NY - 1, 128, 3 * W // 2), BF16),
            vm((NX, NY, 32, 3 * W // 2), BF16),
            vm((NX - 1, NY, 32, 3 * W // 2), BF16),
            vm((128, 3 * W // 2), F32),
            vm((128, 3 * W // 2), F32),
            vm((NX, 32, 3 * W // 2), BF16),
            vm((NX - 1, 32, 3 * W // 2), BF16),
            vm((NY, 32, 3 * W // 2), BF16),
            vm((NY - 1, 32, 3 * W // 2), BF16),
            vm((NZ, 24, 128), F32),
            vm((NZ, 24, 128), F32),
            dma((11,)),
            dma((16,)),
            dma((20,)),
        ],
        compiler_params=pltpu.CompilerParams(
            collective_id=0, has_side_effects=True, vmem_limit_bytes=LIMIT
        ),
        name="layer",
    )(
        pattern.T, halo_owner.reshape(1, HR), halo_row.reshape(1, HR),
        query, keys, values, grad_attn, nodes_in, w_query, w_key, w_value,
    )
    return grad_nodes, jnp.transpose(grad_weights, (1, 0, 2))


def solution(mesh):
    in_specs = (
        P("graph", None),
        P("graph", "mp"),
        P("graph", "mp"),
        P("graph", "mp"),
        P("graph", "mp"),
        P(None, "mp"),
        P(None, "mp"),
        P(None, "mp"),
        P("graph", None),
        P("graph"),
        P("graph", None),
    )
    out_specs = (P("graph", "mp"), P("graph", None, "mp"))
    return jax.shard_map(
        on_device, mesh=mesh, in_specs=in_specs, out_specs=out_specs, check_vma=False
    )
```

time: 88.1 us -> 72.2 us (0.82)
  Pallas kernels: 83.2 us -> 68.4 us
    pallas_call x1, Pallas kernels: 83.2 us -> 68.4 us  [on_device(): pl.pallas_call(layer_kernel, out_shape=(jax.ShapeDtypeStruct((ROWS, W), B...]
    pallas_call x1 -> x0, local copies, waits for them, and re-layouts: 1.32 us -> none  [on_device(): pl.pallas_call(layer_kernel, out_shape=(jax.ShapeDtypeStruct((ROWS, W), B...]
    unnamed x1 -> x4, local copies, waits for them, and re-layouts: 2.26 us -> 2.87 us
where the time goes in v3:
time: 72.2 us; the launch traced here: 71.9 us
  Pallas kernels  68.4 us (95%)
  local copies, waits for them, and re-layouts  2.87 us (4%)
    pallas_call x1, Pallas kernels, on_device(): pl.pallas_call(layer_kernel, out_shape=(jax.ShapeDtypeStruct((ROWS, W), B...  68.4 us
    unnamed x4, local copies, waits for them, and re-layouts  2.87 us

profile of v3, /device:TPU:2, one launch (start us, length us, event | category | flops | bytes accessed | tf_op | source)
XLA Modules:
  0.0 71.9 jit_solution(6745343405742030324)
XLA Ops:
  0.6 68.4 %layer.1 = (bf16[2048,256]{1,0:T(8,128)(2,1)}, f32[3,4,256]{2,1,0:T(4,128)}) custom-call(s32[2,16]{1,0:T(2,128)} %bitcast.5, s32[1,256]{1,0:T(1,128)} %bitcast.6, s32[1,256]{1,0:T(1,128)} %bitcast.7, bf16[2048,256]{1,0:T(8,128)(2,1)} %query_hbm.1, bf16[2048,256]{1,0:T(8,128)(2,1)} %keys_hbm.1, bf16[2048,256]{1,0:T(8,128)(2,1)} %values_hbm.1, ...), custom_call_target="tpu_custom_call" | custom-call | tf_op jit(solution)/shard_map/layer/pallas_call | solution.py:612
  69.0 0.0 copy-start
  69.1 2.3 %copy.15 = bf16[2048,256]{1,0:T(8,128)(2,1)} copy(bf16[2048,256]{1,0:T(8,128)(2,1)} %get-tuple-element.8) | data formatting | bytes 2097152
  71.3 0.0 copy-done
  71.3 0.6 copy.16
Async XLA Ops:
  69.0 2.3 %copy-start = (f32[3,4,256]{2,1,0:T(4,128)S(1)}, f32[3,4,256]{2,1,0:T(4,128)}, u32[]{:S(2)}) copy-start(f32[3,4,256]{2,1,0:T(4,128)} %get-tuple-element.5) | copy-start | bytes 36868

commit v4 on v3

--- a/solution.py
+++ b/solution.py
@@ -193,21 +193,30 @@
 
     loads[0].wait()
     loads[1].wait()
-    for j in range(CAP):
-        pick = onehot(asked[j] == iota((NG, ROWS), 1))
+    for part in range(2):
+        ks = slice(part * HALF, (part + 1) * HALF)
+        pick = jnp.concatenate(
+            [onehot(asked[j][ks] == iota((HALF, ROWS), 1)) for j in range(CAP)], 0
+        )
         part_k = dot(pick, kbuf[...])
         part_v = dot(pick, vbuf[...])
-        for c in range(2):
-            fst[pl.ds(4 * j + c, NG, stride=16), :] = part_k[:, c * 128 : (c + 1) * 128]
-            fst[pl.ds(4 * j + 2 + c, NG, stride=16), :] = part_v[:, c * 128 : (c + 1) * 128]
-    kv_send[...] = fst[...].reshape(NG, 16, 128).astype(BF16)
-
-    @pl.loop(0, NPLANE)
-    def _(dp):
-        base = lax.rem(plane - dp + NPLANE, NPLANE) * NZ
-        for dz in range(1, NZ):
-            k = dp * NZ + dz
-            send(kv_send.at[k], kv_recv.at[k], ssem.at[2], rsem.at[2], (base + z_down[dz], mp))
+        for j in range(CAP):
+            rows = slice(j * HALF, (j + 1) * HALF)
+            first = part * HALF * 16 + 4 * j
+            for c in range(2):
+                cols = slice(c * 128, (c + 1) * 128)
+                fst[pl.ds(first + c, HALF, stride=16), :] = part_k[rows, cols]
+                fst[pl.ds(first + 2 + c, HALF, stride=16), :] = part_v[rows, cols]
+        kv_send[ks] = (
+            fst[part * HALF * 16 : (part + 1) * HALF * 16, :].reshape(HALF, 16, 128).astype(BF16)
+        )
+
+        @pl.loop(part * NPLANE // 2, (part + 1) * NPLANE // 2)
+        def _(dp):
+            base = lax.rem(plane - dp + NPLANE, NPLANE) * NZ
+            for dz in (4, 3, 5, 2, 6, 1, 7):
+                k = dp * NZ + dz
+                send(kv_send.at[k], kv_recv.at[k], ssem.at[2], rsem.at[2], (base + z_down[dz], mp))
 
     @pl.loop(1, NPLANE)
     def _(dp):
@@ -278,9 +287,11 @@
 
     def scores(step, h):
         rows = slice(2 * h * BLK, 2 * (h + 1) * BLK)
+        first = h // 2 * 128
+        pair = slice(first, first + 128)
         return (
-            dot(far_kv[:, 0:W], qms[step, rows, :], NT),
-            dot(far_kv[:, W : 2 * W], gms[step, rows, :], NT),
+            dot(far_kv[:, pair], qms[step, rows, pair], NT),
+            dot(far_kv[:, W + first : W + first + 128], gms[step, rows, pair], NT),
         )
 
     def soften(step, h, bias, s_far, d_far, buf):
@@ -314,7 +325,12 @@
         first = pl.multiple_of(step * 2 * BLK, 2 * BLK)
         if part < 2:
             stacked = (qms, gms)[part]
-            far_acc[:, part * W : (part + 1) * W] += dot(buf[part, BLK:, :], stacked[step])
+            for pair in range(2):
+                span = slice(pair * 4 * BLK, (pair + 1) * 4 * BLK)
+                lane = part * W + pair * 128
+                far_acc[:, lane : lane + 128] += dot(
+                    buf[part, BLK:, span], stacked[step, span, pair * 128 : (pair + 1) * 128]
+                )
         elif part == 2:
             pieces = []
             for h in range(HEADS_LOCAL):

time: 72.2 us -> 71.8 us (level)
  Pallas kernels: 68.4 us -> 67.6 us
    pallas_call x1, Pallas kernels: 68.4 us -> 67.6 us  [on_device(): pl.pallas_call(layer_kernel, out_shape=(jax.ShapeDtypeStruct((ROWS, W), B...]
where the time goes in v4:
time: 71.8 us; the launch traced here: 71.1 us
  Pallas kernels  67.6 us (94%)
  local copies, waits for them, and re-layouts  2.87 us (4%)
    pallas_call x1, Pallas kernels, on_device(): pl.pallas_call(layer_kernel, out_shape=(jax.ShapeDtypeStruct((ROWS, W), B...  67.6 us
    unnamed x4, local copies, waits for them, and re-layouts  2.87 us

profile of v4, /device:TPU:2, one launch (start us, length us, event | category | flops | bytes accessed | tf_op | source)
XLA Modules:
  0.0 71.1 jit_solution(6966662040961793584)
XLA Ops:
  0.6 67.6 %layer.1 = (bf16[2048,256]{1,0:T(8,128)(2,1)}, f32[3,4,256]{2,1,0:T(4,128)}) custom-call(s32[2,16]{1,0:T(2,128)} %bitcast.5, s32[1,256]{1,0:T(1,128)} %bitcast.6, s32[1,256]{1,0:T(1,128)} %bitcast.7, bf16[2048,256]{1,0:T(8,128)(2,1)} %query_hbm.1, bf16[2048,256]{1,0:T(8,128)(2,1)} %keys_hbm.1, bf16[2048,256]{1,0:T(8,128)(2,1)} %values_hbm.1, ...), custom_call_target="tpu_custom_call" | custom-call | tf_op jit(solution)/shard_map/layer/pallas_call | solution.py:628
  68.2 0.0 copy-start
  68.2 2.3 %copy.15 = bf16[2048,256]{1,0:T(8,128)(2,1)} copy(bf16[2048,256]{1,0:T(8,128)(2,1)} %get-tuple-element.8) | data formatting | bytes 2097152
  70.5 0.0 copy-done
  70.5 0.6 copy.16
Async XLA Ops:
  68.2 2.3 %copy-start = (f32[3,4,256]{2,1,0:T(4,128)S(1)}, f32[3,4,256]{2,1,0:T(4,128)}, u32[]{:S(2)}) copy-start(f32[3,4,256]{2,1,0:T(4,128)} %get-tuple-element.5) | copy-start | bytes 36868

commit v5 on v4

--- a/solution.py
+++ b/solution.py
@@ -163,7 +163,7 @@
     k_r = dplane_r * NZ + dz_r
     pl.semaphore_wait(barrier, NZ - 1 + NPLANE - 1 + 1)
 
-    for dz in range(1, NZ):
+    for dz in (4, 3, 5, 2, 6, 1, 7):
         send(s1.at[dz], r1.at[dz], ssem.at[0], rsem.at[0], (plane * NZ + z_up[dz], mp))
     r1[0] = s1[0]
     wait_bytes(r1.at[pl.ds(0, NZ - 1)], rsem.at[0])
@@ -493,7 +493,7 @@
     @pl.loop(0, NPLANE // 2)
     def _(i):
         base = lax.rem(plane + first_plane + i, NPLANE) * NZ
-        for dz in range(1, NZ):
+        for dz in (4, 3, 5, 2, 6, 1, 7):
             k = i * NZ + dz
             send(z_send.at[k], z_recv.at[k], ssem.at[9], rsem.at[9], (base + z_up[dz], mp))
 
@@ -552,7 +552,7 @@
             zz_send[zz, 4 * c + 12 : 4 * c + 16, :] = own_b[
                 4 * zz : 4 * zz + 4, c * 128 : (c + 1) * 128
             ]
-    for d in range(1, NZ):
+    for d in (4, 3, 5, 2, 6, 1, 7):
         send(
             zz_send.at[z_up[d]], zz_recv.at[d], ssem.at[12], rsem.at[12], (plane * NZ + z_up[d], mp)
         )

time: 71.8 us -> 71.8 us (level)
  no operation moved by 1% of the time
where the time goes in v5:
time: 71.8 us; the launch traced here: 70.8 us
  Pallas kernels  67.3 us (94%)
  local copies, waits for them, and re-layouts  2.87 us (4%)
    pallas_call x1, Pallas kernels, on_device(): pl.pallas_call(layer_kernel, out_shape=(jax.ShapeDtypeStruct((ROWS, W), B...  67.3 us
    unnamed x4, local copies, waits for them, and re-layouts  2.87 us

profile of v5, /device:TPU:2, one launch (start us, length us, event | category | flops | bytes accessed | tf_op | source)
XLA Modules:
  0.0 70.8 jit_solution(8187599572914650955)
XLA Ops:
  0.6 67.3 %layer.1 = (bf16[2048,256]{1,0:T(8,128)(2,1)}, f32[3,4,256]{2,1,0:T(4,128)}) custom-call(s32[2,16]{1,0:T(2,128)} %bitcast.5, s32[1,256]{1,0:T(1,128)} %bitcast.6, s32[1,256]{1,0:T(1,128)} %bitcast.7, bf16[2048,256]{1,0:T(8,128)(2,1)} %query_hbm.1, bf16[2048,256]{1,0:T(8,128)(2,1)} %keys_hbm.1, bf16[2048,256]{1,0:T(8,128)(2,1)} %values_hbm.1, ...), custom_call_target="tpu_custom_call" | custom-call | tf_op jit(solution)/shard_map/layer/pallas_call | solution.py:628
  67.9 0.0 copy-start
  68.0 2.3 %copy.15 = bf16[2048,256]{1,0:T(8,128)(2,1)} copy(bf16[2048,256]{1,0:T(8,128)(2,1)} %get-tuple-element.8) | data formatting | bytes 2097152
  70.2 0.0 copy-done
  70.2 0.6 copy.16
Async XLA Ops:
  67.9 2.3 %copy-start = (f32[3,4,256]{2,1,0:T(4,128)S(1)}, f32[3,4,256]{2,1,0:T(4,128)}, u32[]{:S(2)}) copy-start(f32[3,4,256]{2,1,0:T(4,128)} %get-tuple-element.5) | copy-start | bytes 36868
